TPU v7x, 512 devices: a whole 4x4x16 slice. The times are simulated.
512 devices in a mesh: dp: 32 (over z_hi, x, y), expert: 16 (over z_lo, core).
Axes of the slice: x: 4, y: 4, z: 16 (z_hi: 2, z_lo: 8; z = z_hi * 8 + z_lo), core: 2. Of those that a mesh axis runs over, the one named last changes fastest.
Arguments:
- frames: bfloat16 [12288, 1024], P('dp'), may hold values from -6 to 6
- norm_gain: float32 [1024], replicated, may hold values from 0.1 to 1.9
- router: float32 [1024, 32], replicated, may hold values from -0.1875 to 0.1875
- routes: int32 [12288, 2], P('dp'), may hold values from 0 to 31, all different within a row; in each aligned block of 384 rows (0 to 383, 384 to 767, ...) at most 32 rows name the same one
- w_in: bfloat16 [32, 1024, 4096], P('dp', None, 'expert'), may hold values from -0.25 to 0.25
- w_out: bfloat16 [32, 4096, 1024], P('dp', 'expert'), may hold values from -0.125 to 0.125
- cotangent: bfloat16 [12288, 1024], P('dp', 'expert'), may hold values from -6 to 6
Outputs:
- mixed_out: bfloat16 [12288, 1024], P('dp', 'expert')
- d_frames: bfloat16 [12288, 1024], P('dp', 'expert')
- d_gain: float32 [1024], P('expert')
- d_router: float32 [1024, 32], replicated
- grad_in: bfloat16 [32, 1024, 4096], P('dp', None, 'expert')
- grad_out: bfloat16 [32, 4096, 1024], P('dp', 'expert')
Inputs may be any that keep to these rules, and one draw needn't show every extreme that they name: `routes`: each row names 2 different experts; among the rows of one device no expert is named more than 32 times, a bound that some block reaches.
All inputs are finite; a program needn't handle non-finite values.
Results may differ from a plain program's by a relative error of at most 0.023.
Values may be sent and summed in bfloat16 or wider, within the bound.
A program may use at most 64 MiB of HBM per device.

v0:
```python
import jax
import jax.numpy as jnp
from jax import lax
from jax.sharding import PartitionSpec as P

epsilon = 1e-05


def silu_slope(hidden):
    sigmoid_h = jax.nn.sigmoid(hidden)
    return sigmoid_h * (1.0 + hidden * (1.0 - sigmoid_h))


def shards(frames, norm_gain, router, routes, w_in, w_out, cotangent):
    tok_rows, width_all = frames.shape
    experts = router.shape[1]
    top_count = routes.shape[1]
    dp_size = lax.axis_size("dp")
    column = lax.axis_index("expert")
    col_width = cotangent.shape[1]
    col_start = column * col_width
    capacity = 4 * top_count * tok_rows // (3 * experts)
    values = frames.astype(jnp.float32)
    centred = values - jnp.mean(values, axis=1, keepdims=True)
    inverse = lax.rsqrt(jnp.mean(centred * centred, axis=1, keepdims=True) + epsilon)
    scaled = centred * inverse
    normed = (scaled * norm_gain).astype(jnp.bfloat16)
    logits = jnp.dot(normed.astype(jnp.float32), router, precision=lax.Precision.HIGHEST)
    gate_values = jax.nn.sigmoid(jnp.take_along_axis(logits, routes, axis=1))
    flat_ids = routes.reshape(tok_rows * top_count)
    expert_ids = jnp.arange(experts, dtype=jnp.int32)
    onehot = (flat_ids[:, None] == expert_ids[None, :]).astype(jnp.float32)
    entries = tok_rows * top_count
    lower_mask = (jnp.arange(entries)[:, None] > jnp.arange(entries)[None, :]).astype(jnp.float32)
    earlier = jnp.dot(lower_mask, onehot, precision=lax.Precision.HIGHEST)
    slot_ids = jnp.sum(earlier * onehot, axis=1).astype(jnp.int32)
    position = flat_ids * capacity + slot_ids
    total_rows = experts * capacity
    sendbuf = (
        jnp.zeros((total_rows, width_all), jnp.bfloat16)
        .at[position]
        .set(jnp.repeat(normed, top_count, axis=0))
    )
    arrived = lax.all_to_all(
        sendbuf.reshape(experts, capacity, width_all), "dp", split_axis=0, concat_axis=0, tiled=True
    )
    arrived = arrived.reshape(dp_size * capacity, width_all)
    weight_in = w_in[0]
    weight_out = w_out[0]
    hidden = jnp.dot(arrived, weight_in, preferred_element_type=jnp.float32)
    active = jax.nn.silu(hidden).astype(jnp.bfloat16)
    partial_value = jnp.dot(active, weight_out, preferred_element_type=jnp.float32)
    expert_cols = lax.psum_scatter(
        partial_value.astype(jnp.bfloat16), "expert", scatter_dimension=1, tiled=True
    )
    flat_back = lax.all_to_all(
        expert_cols.reshape(dp_size, capacity, col_width),
        "dp",
        split_axis=0,
        concat_axis=0,
        tiled=True,
    )
    flat_back = flat_back.reshape(total_rows, col_width)
    picked = (
        jnp.take(flat_back, position, axis=0)
        .reshape(tok_rows, top_count, col_width)
        .astype(jnp.float32)
    )
    value_cols = lax.dynamic_slice_in_dim(values, col_start, col_width, 1)
    mixed_out = (value_cols + 0.5 * jnp.sum(gate_values[:, :, None] * picked, axis=1)).astype(
        jnp.bfloat16
    )
    cot_values = cotangent.astype(jnp.float32)
    grad_rows = (0.5 * gate_values[:, :, None] * cot_values[:, None, :]).astype(jnp.bfloat16)
    grad_buffer = (
        jnp.zeros((total_rows, col_width), jnp.bfloat16)
        .at[position]
        .set(grad_rows.reshape(entries, col_width))
    )
    grads_cols = lax.all_to_all(
        grad_buffer.reshape(experts, capacity, col_width),
        "dp",
        split_axis=0,
        concat_axis=0,
        tiled=True,
    )
    grads_full = lax.all_gather(
        grads_cols.reshape(dp_size * capacity, col_width), "expert", axis=1, tiled=True
    )
    upstream = jnp.dot(grads_full, weight_out.T, preferred_element_type=jnp.float32)
    d_hidden = (upstream * silu_slope(hidden)).astype(jnp.bfloat16)
    grad_out = jnp.dot(active.T, grads_full, preferred_element_type=jnp.float32).astype(
        jnp.bfloat16
    )
    grad_in = jnp.dot(arrived.T, d_hidden, preferred_element_type=jnp.float32).astype(jnp.bfloat16)
    back_partial = jnp.dot(d_hidden, weight_in.T, preferred_element_type=jnp.float32)
    back_cols = lax.psum_scatter(
        back_partial.astype(jnp.bfloat16), "expert", scatter_dimension=1, tiled=True
    )
    back_rows = lax.all_to_all(
        back_cols.reshape(dp_size, capacity, col_width),
        "dp",
        split_axis=0,
        concat_axis=0,
        tiled=True,
    )
    back_rows = back_rows.reshape(total_rows, col_width)
    d_moe = jnp.sum(
        jnp.take(back_rows, position, axis=0)
        .reshape(tok_rows, top_count, col_width)
        .astype(jnp.float32),
        axis=1,
    )
    gate_part = 0.5 * jnp.sum(cot_values[:, None, :] * picked, axis=2)
    gain_cols = lax.dynamic_slice_in_dim(norm_gain, col_start, col_width, 0)
    scaled_cols = lax.dynamic_slice_in_dim(scaled, col_start, col_width, 1)
    selector = (routes[:, :, None] == expert_ids[None, None, :]).astype(jnp.float32)
    d_gate = lax.psum(gate_part, "expert")
    d_chosen = d_gate * gate_values * (1.0 - gate_values)
    d_logits = jnp.sum(selector * d_chosen[:, :, None], axis=1)
    router_cols = lax.dynamic_slice_in_dim(router, col_start, col_width, 0)
    d_normed = d_moe + jnp.dot(d_logits, router_cols.T, precision=lax.Precision.HIGHEST)
    d_scaled = d_normed * gain_cols
    first_sum, second_sum = lax.psum(
        (jnp.sum(d_scaled, axis=1), jnp.sum(d_scaled * scaled_cols, axis=1)), "expert"
    )
    d_frames = cot_values + inverse * (
        d_scaled - first_sum[:, None] / width_all - scaled_cols * (second_sum[:, None] / width_all)
    )
    gain_total, router_total = lax.psum(
        (
            jnp.sum(d_normed * scaled_cols, axis=0),
            jnp.dot(normed.astype(jnp.float32).T, d_logits, precision=lax.Precision.HIGHEST),
        ),
        "dp",
    )
    d_gain = gain_total / tok_rows
    d_router = router_total / tok_rows
    return (
        mixed_out,
        d_frames.astype(jnp.bfloat16),
        d_gain,
        d_router,
        grad_in.reshape(1, width_all, -1),
        grad_out.reshape(1, -1, width_all),
    )


def solution(mesh):
    placed = (
        P("dp", None),
        P(),
        P(),
        P("dp", None),
        P("dp", None, "expert"),
        P("dp", "expert", None),
        P("dp", "expert"),
    )
    return jax.shard_map(
        shards,
        mesh=mesh,
        in_specs=placed,
        out_specs=(
            P("dp", "expert"),
            P("dp", "expert"),
            P("expert"),
            P(),
            P("dp", None, "expert"),
            P("dp", "expert", None),
        ),
        check_vma=False,
    )
```

profile of v0, /device:TPU:1, one launch (start us, length us, event | category | flops | bytes accessed | tf_op | source)
XLA Modules:
  0.0 1359.8 jit_solution(5535783752299411263)
XLA Ops:
  12.2 2.0 broadcast_in_dim.21
  14.2 3.6 reshape.179
  17.8 8.0 scatter_custom_fusion
  25.8 70.9 %all_to_all.20 = bf16[32,32,1024]{2,1,0:T(8,128)(2,1)S(1)} all-to-all(bf16[32,32,1024]{2,1,0:T(8,128)(2,1)} %bitcast.45), channel_id=1, replica_groups=mesh['dp'=32,'expert'=16] {'dp'}, dimensions={0} | all-to-all | bytes 4194304 | tf_op jit(solution)/shard_map/all_to_all | solution.py:44
  99.8 2.1 convolution_convert_fusion.1
  103.0 146.0 %reduce-scatter.3.cloned.1.call-done = bf16[1024,64]{0,1:T(8,128)(2,1)} async-done(((bf16[1024,1024]{0,1:T(8,128)(2,1)}), bf16[1024,64]{0,1:T(8,128)(2,1)}) %reduce-scatter.3.cloned.1.call-update) | async-done | bytes 131088 | tf_op jit(solution)/shard_map/reduce_scatter | solution.py:53
  250.9 16.4 %all-to-all-start.1 = ((bf16[32,2,1024]{2,1,0:T(2,128)(2,1)}), bf16[32,2,1024]{2,1,0:T(2,128)(2,1)S(1)}, u32[]{:S(2)}, u32[]{:S(2)}) async-start(bf16[32,2,1024]{2,1,0:T(2,128)(2,1)} %reshape.207), calls=%async_computation.2 | async-start | bytes 262144 | tf_op jit(solution)/shard_map/all_to_all | solution.py:56
  268.0 6.3 gather_fusion
  274.7 8.7 all-to-all-done.1
  283.6 1.9 gather_fusion.1
  286.2 47.9 %psum.35 = f32[384,2]{0,1:T(2,128)S(1)} all-reduce(f32[384,2]{0,1:T(2,128)S(1)} %copy.94), channel_id=1, replica_groups=mesh['dp'=32,'expert'=16] {'expert'}, use_global_device_ids=true, to_apply=%region_10.12 | all-reduce | flops 768 | bytes 6144 | tf_op jit(solution)/shard_map/psum | solution.py:118
  334.5 4.9 scatter_custom_fusion.1
  339.6 22.7 %all_to_all.21 = bf16[32,2,1024]{2,1,0:T(2,128)(2,1)S(1)} all-to-all(bf16[32,2,1024]{2,1,0:T(2,128)(2,1)S(1)} %reshape.209), channel_id=1, replica_groups=mesh['dp'=32,'expert'=16] {'dp'}, dimensions={0} | all-to-all | bytes 262144 | tf_op jit(solution)/shard_map/all_to_all | solution.py:80
  364.9 94.9 %all-gather.2.cloned.1.call-done = bf16[1024,1024]{0,1:T(8,128)(2,1)} async-done(((bf16[1024,64]{0,1:T(8,128)(2,1)}), bf16[1024,1024]{0,1:T(8,128)(2,1)}) %all-gather.2.cloned.1.call-update) | async-done | bytes 2097168 | tf_op jit(solution)/shard_map/all_gather | solution.py:87
  459.8 2.8 fusion.1
  463.4 2.1 convolution_convert_fusion
  467.7 528.2 %all-reduce.3.cloned.1.call-done = f32[1024,32]{0,1:T(8,128)} async-done(((f32[1024,32]{0,1:T(8,128)}), f32[1024,32]{0,1:T(8,128)}) %all-reduce.3.cloned.1.call-update) | async-done | bytes 131088 | tf_op jit(solution)/shard_map/psum | solution.py:130
  997.5 115.8 %reduce-scatter.5.cloned.1.call-done = bf16[1024,64]{0,1:T(8,128)(2,1)} async-done(((bf16[1024,1024]{0,1:T(8,128)(2,1)}), bf16[1024,64]{0,1:T(8,128)(2,1)}) %reduce-scatter.5.cloned.1.call-update) | async-done | bytes 131088 | tf_op jit(solution)/shard_map/reduce_scatter | solution.py:97
  1115.2 16.5 %all-to-all-start.3 = ((bf16[32,2,1024]{2,1,0:T(2,128)(2,1)}), bf16[32,2,1024]{2,1,0:T(2,128)(2,1)S(1)}, u32[]{:S(2)}, u32[]{:S(2)}) async-start(bf16[32,2,1024]{2,1,0:T(2,128)(2,1)} %reshape.211), calls=%async_computation.5 | async-start | bytes 262144 | tf_op jit(solution)/shard_map/all_to_all | solution.py:100
  1131.8 2.8 fusion.2
  1136.2 11.7 all-to-all-done.3
  1148.1 1.9 gather_fusion.2
  1152.3 135.1 %psum.38 = f32[64]{0:T(128)S(1)} all-reduce(f32[64]{0:T(128)S(1)} %get-tuple-element.7), channel_id=1, replica_groups=mesh['dp'=32,'expert'=16] {'dp'}, use_global_device_ids=true, to_apply=%region_17.19 | all-reduce | flops 64 | bytes 512 | tf_op jit(solution)/shard_map/psum | solution.py:130
  1290.2 61.4 %all-reduce = (f32[384]{0:T(512)S(1)}, f32[384]{0:T(512)S(1)}) all-reduce(f32[384]{0:T(512)S(1)} %get-tuple-element.8, f32[384]{0:T(512)S(1)} %get-tuple-element.9), channel_id=1, replica_groups=mesh['dp'=32,'expert'=16] {'expert'}, use_global_device_ids=true, to_apply=%region_15.17 | all-reduce | flops 768 | bytes 6144 | tf_op jit(solution)/shard_map/psum | solution.py:124
  (102 shorter events, 30.9 us)
Async XLA Ops:
  7.2 92.6 %copy-start = (bf16[1,256,1024]{2,1,0:T(8,128)(2,1)S(1)}, bf16[1,256,1024]{2,1,0:T(8,128)(2,1)}, u32[]{:S(2)}) copy-start(bf16[1,256,1024]{2,1,0:T(8,128)(2,1)} %param.14) | copy-start | bytes 1572868
  7.2 2.5 copy-start.6
  7.2 241.8 %reduce-scatter.3.cloned.1.call-start = ((), (), s32[]{:S(2)}) async-start(), calls=%async_computation.6 | async-start | bytes 2228224 | tf_op jit(solution)/shard_map/reduce_scatter | solution.py:53
  9.2 1.4 copy-start.13
  25.8 72.3 %copy-start.8 = (bf16[1,1024,256]{2,1,0:T(8,128)(2,1)S(1)}, bf16[1,1024,256]{2,1,0:T(8,128)(2,1)}, u32[]{:S(2)}) copy-start(bf16[1,1024,256]{2,1,0:T(8,128)(2,1)} %param.13) | copy-start | bytes 1572868
  96.7 1.4 copy-start.1
  98.8 1.0 copy-start.15
  101.9 0.7 copy-start.12
  101.9 1.0 copy-start.9
  101.9 165.6 %copy-start.11 = (f32[1024,32]{0,1:T(8,128)S(1)}, f32[1024,32]{0,1:T(8,128)}, u32[]{:S(2)}) copy-start(f32[1024,32]{0,1:T(8,128)} %param.11) | copy-start | bytes 393220
  250.9 32.5 %all-to-all-start.1 = ((bf16[32,2,1024]{2,1,0:T(2,128)(2,1)}), bf16[32,2,1024]{2,1,0:T(2,128)(2,1)S(1)}, u32[]{:S(2)}, u32[]{:S(2)}) async-start(bf16[32,2,1024]{2,1,0:T(2,128)(2,1)} %reshape.207), calls=%async_computation.2 | async-start | bytes 262144 | tf_op jit(solution)/shard_map/all_to_all | solution.py:56
  267.3 192.5 %all-gather.2.cloned.1.call-start = ((), (), s32[]{:S(2)}) async-start(), calls=%async_computation.7 | async-start | bytes 2228224 | tf_op jit(solution)/shard_map/all_gather | solution.py:87
  285.5 77.8 %copy-start.3 = (bf16[768,64]{1,0:T(8,128)(2,1)}, bf16[768,64]{1,0:T(8,128)(2,1)S(1)}, u32[]{:S(2)}) copy-start(bf16[768,64]{1,0:T(8,128)(2,1)S(1)} %gather_fusion.1) | copy-start | bytes 294916
  363.3 632.6 %all-reduce.3.cloned.1.call-start = ((), (), s32[]{:S(2)}) async-start(), calls=%async_computation.9 | async-start | bytes 262144 | tf_op jit(solution)/shard_map/psum | solution.py:130
  364.9 748.5 %reduce-scatter.5.cloned.1.call-start = ((), (), s32[]{:S(2)}) async-start(), calls=%async_computation.8 | async-start | bytes 2228224 | tf_op jit(solution)/shard_map/reduce_scatter | solution.py:97
  462.6 0.8 copy-start.5
  465.5 666.3 %copy-start.2 = (bf16[32,32,1024]{2,1,0:T(8,128)(2,1)S(1)}, bf16[32,32,1024]{2,1,0:T(8,128)(2,1)}, u32[]{:S(2)}) copy-start(bf16[32,32,1024]{2,1,0:T(8,128)(2,1)} %copy-done.1) | copy-start | bytes 6291460
  1115.2 32.6 %all-to-all-start.3 = ((bf16[32,2,1024]{2,1,0:T(2,128)(2,1)}), bf16[32,2,1024]{2,1,0:T(2,128)(2,1)S(1)}, u32[]{:S(2)}, u32[]{:S(2)}) async-start(bf16[32,2,1024]{2,1,0:T(2,128)(2,1)} %reshape.211), calls=%async_computation.5 | async-start | bytes 262144 | tf_op jit(solution)/shard_map/all_to_all | solution.py:100
  1131.8 2.8 copy-start.14
  1131.8 2.8 copy-start.16
  1136.2 13.8 %copy-start.4 = (bf16[768,64]{1,0:T(8,128)(2,1)S(1)}, bf16[768,64]{1,0:T(8,128)(2,1)}, u32[]{:S(2)}) copy-start(bf16[768,64]{1,0:T(8,128)(2,1)} %copy-done.3) | copy-start | bytes 294916
  1136.2 151.8 %copy-start.7 = (f32[384,2]{1,0:T(8,128)S(1)}, f32[384,2]{1,0:T(8,128)}, u32[]{:S(2)}) copy-start(f32[384,2]{1,0:T(8,128)} %copy.84) | copy-start | bytes 9220
  1150.0 201.6 %copy-start.10 = (bf16[384,64]{0,1:T(8,128)(2,1)S(1)}, bf16[384,64]{0,1:T(8,128)(2,1)}, u32[]{:S(2)}) copy-start(bf16[384,64]{0,1:T(8,128)(2,1)} %param.15) | copy-start | bytes 147460
Sparse Core Ops, SparseCore 0:
  102.1 146.8 reduce-scatter.2
  363.4 96.3 all-gather.1
  463.3 532.6 all-reduce.2
  998.8 114.4 reduce-scatter.4
where the time goes:
time: 1360 us
  waiting for transfers between devices  905 us (67%)
  blocking collectives  338 us (25%)
  local copies, waits for them, and re-layouts  37.3 us (3%)
  starting transfers between devices  33.2 us (2%)
  other arithmetic  15.8 us (1%)
  matrix products  15.7 us (1%)
  between operations  14.2 us (1%)
    psum x1, waiting for transfers between devices, shards(): lax.psum((jnp.sum(d_normed * scaled_cols, axis=0), jnp.dot(normed.astype(...  528 us
    reduce_scatter x1, waiting for transfers between devices, shards(): lax.psum_scatter(partial_value.astype(jnp.bfloat16), 'expert', scatter_di...  146 us
    psum x1, blocking collectives, shards(): lax.psum((jnp.sum(d_normed * scaled_cols, axis=0), jnp.dot(normed.astype(...  135 us
    reduce_scatter x1, waiting for transfers between devices, shards(): lax.psum_scatter(back_partial.astype(jnp.bfloat16), 'expert', scatter_dim...  116 us
    all_gather x1, waiting for transfers between devices, shards(): lax.all_gather(grads_cols.reshape(dp_size * capacity, col_width), 'expert...  94.9 us
    all_to_all x1, blocking collectives, shards(): lax.all_to_all(sendbuf.reshape(experts, capacity, width_all), 'dp', split...  70.9 us
    psum x1, blocking collectives, shards(): lax.psum((jnp.sum(d_scaled, axis=1), jnp.sum(d_scaled * scaled_cols, axis...  61.4 us
    psum x1, blocking collectives, shards(): d_gate = lax.psum(gate_part, 'expert')  47.9 us
  transfers between devices with their start and end apart: 6, of which 6 were waited for; matrix products, arithmetic and copies ran while one was open for 2% of the time, Pallas kernels for 0%

commit v1 on v0

v1 whole, which is shorter than its diff:
```python
import functools

import jax
import jax.numpy as jnp
from jax import lax
from jax.experimental import pallas as pl
from jax.experimental.pallas import tpu as pltpu
from jax.sharding import PartitionSpec as P

EPS = 1e-05
F32 = jnp.float32
BF16 = jnp.bfloat16
MESH = pl.DeviceIdType.MESH
NN = (((1,), (0,)), ((), ()))
NT = (((1,), (1,)), ((), ()))


def dot(a, b, dims=NN):
    return lax.dot_general(a, b, dims, preferred_element_type=F32)


def loop(lo, hi, body):
    def step(i, carry):
        body(i)
        return carry

    lax.fori_loop(lo, hi, step, 0)


def kernel(
    dims,
    frames,
    gain,
    routerT,
    routesT,
    w_in,
    w_out,
    cot,
    mixed,
    dfr,
    vout,
    gin,
    gout,
    rt,
    nb,
    cotb,
    sibcot,
    stats,
    p0t,
    p1t,
    pcomb,
    send_n,
    send_c,
    rows_a,
    rows_c,
    ga_t,
    d_t,
    prodb,
    retb,
    sib_p,
    sib_r,
    got_p,
    got_r,
    part,
    ring,
    scal,
    vw,
    sibvw,
    vz,
    vp,
    tail,
    sib_s,
    sib_q,
    rt_sem,
    nrm_s,
    nrm_q,
    cot_r,
    cot_l,
    cot_q,
    xy_s,
    xy_q,
    rs_s,
    rs_q,
    sc_s,
    sc_q,
    vz_s,
    vz_q,
):
    X, Y, ZL = dims
    NP = X * Y
    NZ = 2 * ZL
    T, D = frames.shape
    SL = send_n.shape[0]
    CAP = SL // NP
    E = routerT.shape[0]
    W = 128
    dp = lax.axis_index("dp")
    ex = lax.axis_index("expert")
    p = lax.rem(dp, NP)
    zh = dp // NP
    zl = ex // 2
    c = lax.rem(ex, 2)
    z = zh * ZL + zl
    x = p // Y
    y = lax.rem(p, Y)
    r = lax.rem(z + NZ - ZL * c, NZ)
    own = r < ZL
    sib_id = (dp, zl * 2 + 1 - c)

    def z_id(to):
        return ((to // ZL) * NP + p, lax.rem(to, ZL) * 2 + c)

    right = z_id(lax.rem(z + 1, NZ))
    left = z_id(lax.rem(z + NZ - 1, NZ))

    def plane(k, sign):
        px = lax.rem(x + X + sign * (k // Y), X)
        py = lax.rem(y + Y + sign * lax.rem(k, Y), Y)
        return px * Y + py

    def plane_id(k):
        return (zh * NP + plane(k, 1), ex)

    def remote(src, dst, ssem, rsem, to):
        return pltpu.make_async_remote_copy(
            src_ref=src, dst_ref=dst, send_sem=ssem, recv_sem=rsem, device_id=to, device_id_type=MESH
        )

    def sib(src, dst, i):
        return remote(src, dst, sib_s.at[i], sib_q.at[i], sib_id)

    barrier = pltpu.get_barrier_semaphore()

    def greet(to):
        pl.semaphore_signal(barrier, inc=1, device_id=to, device_id_type=MESH)

    greet(sib_id)
    loop(1, NP, lambda k: greet(plane_id(k)))
    loop(1, NZ, lambda k: greet(z_id(lax.rem(z + k, NZ))))

    @pl.when(own)
    def _():
        step = T // 8

        def norm(i):
            at = pl.ds(pl.multiple_of(i * step, step), step)
            values = frames[at, :].astype(F32)
            mean = jnp.mean(values, axis=1, keepdims=True)
            centred = values - mean
            inverse = lax.rsqrt(jnp.mean(centred * centred, axis=1, keepdims=True) + EPS)
            normed = (centred * inverse * gain[...]).astype(BF16)
            for s in range(ZL):
                nb[s, at, :] = normed[:, s * W : (s + 1) * W]
            stats[0, at, :] = jnp.broadcast_to(mean, (step, W))
            stats[1, at, :] = jnp.broadcast_to(inverse, (step, W))

        loop(0, 8, norm)
        rt[...] = routesT[...]

    pl.semaphore_wait(barrier, NP + NZ - 1)

    cot_copy = sib(cot, sibcot, 0)
    rt_copy = remote(rt, rt, rt_sem.at[0], rt_sem.at[1], z_id(lax.rem(z + ZL, NZ)))

    def nrm(s, to):
        return remote(nb.at[s], nb.at[s], nrm_s.at[s], nrm_q.at[s], to)

    def cot_piece(s, sems, to):
        return remote(cotb.at[s], cotb.at[s], sems.at[s], cot_q.at[s], to)

    def cot_step(j, run):
        piece = lax.rem(r + NZ - j, NZ)

        @pl.when(piece < ZL)
        def _():
            s = lax.rem(piece, ZL)
            if run:
                pl.when(j >= 1)(lambda: cot_piece(s, cot_r, right).wait_recv())
            pl.when(j < ZL)(
                lambda: cot_piece(s, cot_r, right).start()
                if run
                else cot_piece(s, cot_r, right).wait_send()
            )

        other = lax.rem(r + j, NZ)

        @pl.when((other < ZL) & (j < ZL))
        def _():
            s = lax.rem(other, ZL)
            if run:
                pl.when(j >= 1)(lambda: cot_piece(s, cot_l, left).wait_recv())
            pl.when(j < ZL - 1)(
                lambda: cot_piece(s, cot_l, left).start()
                if run
                else cot_piece(s, cot_l, left).wait_send()
            )

    def positions():
        r0 = rt[0:1, :].astype(F32)
        r1 = rt[1:2, :].astype(F32)
        lanes = lax.broadcasted_iota(jnp.int32, (E, T), 0).astype(F32)
        e0 = jnp.where(lanes == r0, 1.0, 0.0)
        e1 = jnp.where(lanes == r1, 1.0, 0.0)
        before = lax.broadcasted_iota(jnp.int32, (T, T), 0) < lax.broadcasted_iota(
            jnp.int32, (T, T), 1
        )
        counts = dot((e0 + e1).astype(BF16), jnp.where(before, 1.0, 0.0).astype(BF16))
        base = (zh * NP).astype(F32)
        for rk, ek, pt, first in ((r0, e0, p0t, True), (r1, e1, p1t, False)):
            slot = jnp.sum(ek * counts, axis=0, keepdims=True)
            pos = (rk - base) * CAP + slot
            posc = jnp.transpose(jnp.broadcast_to(pos, (W, T)))
            for b in range(SL // W):
                down = (lax.broadcasted_iota(jnp.int32, (W, T), 0) + b * W).astype(F32)
                pt[b * W : (b + 1) * W, :] = jnp.where(down == pos, 1.0, 0.0).astype(BF16)
                across = (lax.broadcasted_iota(jnp.int32, (T, W), 1) + b * W).astype(F32)
                hit = jnp.where(across == posc, 1.0, 0.0).astype(BF16)
                if first:
                    pcomb[:, b * W : (b + 1) * W] = hit
                else:
                    pcomb[:, b * W : (b + 1) * W] += hit

    def xy(a, src, dst, at, k):
        return remote(
            src.at[pl.ds(pl.multiple_of(plane(k, 1) * CAP, CAP), CAP)],
            dst.at[pl.ds(pl.multiple_of(at + p * CAP, CAP), CAP)],
            xy_s.at[a, k],
            xy_q.at[a, k],
            plane_id(k),
        )

    def xy_arrival(a, dst, at, k):
        here = dst.at[pl.ds(pl.multiple_of(at + plane(k, -1) * CAP, CAP), CAP)]
        return remote(here, here, xy_s.at[a, k], xy_q.at[a, k], plane_id(k))

    def dispatch(a, pieces, send, dst):
        pt = p0t[...] + p1t[...]

        def one(s):
            send[:, pl.ds(pl.multiple_of(s * W, W), W)] = dot(pt, pieces[s]).astype(BF16)

        loop(0, ZL, one)
        loop(1, NP, lambda k: xy(a, send, dst, c * SL, k).start())
        mine = pl.ds(pl.multiple_of(p * CAP, CAP), CAP)
        dst[pl.ds(pl.multiple_of(c * SL + p * CAP, CAP), CAP), :] = send[mine, :]

    @pl.when(own)
    def _():
        rt_copy.start()
        pl.when(r == ZL - 1)(lambda: loop(0, ZL, lambda s: nrm(s, right).start()))
        pl.when(r == 0)(lambda: loop(0, ZL, lambda s: nrm(s, left).start()))
        cot_copy.wait_recv()
        one, two = cot[...], sibcot[...]

        @pl.when(c == 0)
        def _():
            cotb[r, :, :] = jnp.concatenate([one, two], axis=1)

        @pl.when(c == 1)
        def _():
            cotb[r, :, :] = jnp.concatenate([two, one], axis=1)

        cot_step(0, True)
        positions()
        dispatch(0, nb, send_n, rows_a)
        loop(1, ZL + 1, lambda j: cot_step(j, True))

    @pl.when(jnp.logical_not(own))
    def _():
        cot_copy.start()
        rt_copy.wait_recv()
        positions()

        def step(i):
            near = r < ZL + ZL // 2

            @pl.when(near)
            def _():
                nrm(i, right).wait_recv()
                pl.when(r < ZL + ZL // 2 - 1)(lambda: nrm(i, right).start())

            @pl.when(jnp.logical_not(near))
            def _():
                nrm(i, left).wait_recv()
                pl.when(r > ZL + ZL // 2)(lambda: nrm(i, left).start())

            cot_step(i + 1, True)

        loop(0, ZL, step)
        dispatch(0, nb, send_n, rows_a)

    dispatch(1, cotb, send_c, rows_c)

    half = pl.ds(pl.multiple_of(c * SL, SL), SL)
    a_copy = sib(rows_a.at[half], rows_a.at[half], 1)
    c_copy = sib(rows_c.at[half], rows_c.at[half], 2)
    loop(1, NP, lambda k: xy_arrival(0, rows_a, c * SL, k).wait_recv())
    a_copy.start()
    loop(1, NP, lambda k: xy_arrival(1, rows_c, c * SL, k).wait_recv())
    c_copy.start()

    gain_hi = gain[...].astype(BF16)
    gain_lo = (gain[...] - gain_hi.astype(F32)).astype(BF16)
    weight_in = w_in[...]
    weight_out = w_out[...]
    gw = (
        dot(jnp.broadcast_to(gain_hi, (16, D)), weight_in)
        + dot(jnp.broadcast_to(gain_lo, (16, D)), weight_in)
    )[0:1, :]
    router_row = routerT[pl.ds(dp, 1), :]
    router_hi = router_row.astype(BF16)
    router_lo = (router_row - router_hi.astype(F32)).astype(BF16)
    router_hi = jnp.broadcast_to(router_hi, (16, D))
    router_lo = jnp.broadcast_to(router_lo, (16, D))
    vw[...] = jnp.zeros_like(vw)
    RT = 128
    lane = lax.broadcasted_iota(jnp.int32, (RT, W), 1)

    def expert_tile(i):
        at = pl.ds(pl.multiple_of(i * RT, RT), RT)
        arrived = rows_a[at, :]
        cots = rows_c[at, :]
        hidden = dot(arrived, weight_in)
        logit = dot(arrived, router_hi, NT) + dot(arrived, router_lo, NT)
        gate = jax.nn.sigmoid(logit[:, 0:1])
        sig = jax.nn.sigmoid(hidden)
        active = hidden * sig
        up = dot(cots, weight_out, NT) * (0.5 * gate)
        ga = active.astype(BF16).astype(F32) * (0.5 * gate)
        dh = up * (sig * (1.0 + hidden * (1.0 - sig)))
        dh_b = dh.astype(BF16)
        ga_b = ga.astype(BF16)
        ga_t[:, at] = jnp.transpose(ga).astype(BF16)
        d_t[:, at] = jnp.transpose(dh).astype(BF16)
        dgg = jnp.sum(up * active, axis=1, keepdims=True)
        s1 = jnp.sum(dh * gw, axis=1, keepdims=True)
        s2 = jnp.sum(dh * hidden, axis=1, keepdims=True)
        prodb[at, :] = dot(ga_b, weight_out).astype(BF16)
        back = dot(dh_b, weight_in, NT)
        retb[at, 0:D] = back.astype(BF16)
        retb[at, D : D + W] = jnp.where(
            lane == 0, dgg, jnp.where(lane == 1, s1, jnp.where(lane == 2, s2, 0.0))
        ).astype(BF16)
        wide = arrived.astype(F32)
        v = jnp.sum(wide * (dgg * (1.0 - gate)), axis=0, keepdims=True)
        w = jnp.sum(wide * back, axis=0, keepdims=True)
        for b in range(D // W):
            vw[0, b : b + 1, :] += v[:, b * W : (b + 1) * W]
            vw[1, b : b + 1, :] += w[:, b * W : (b + 1) * W]

    tiles = SL // RT
    away = pl.ds(pl.multiple_of((1 - c) * SL, SL), SL)
    p_copy = sib(prodb.at[away], sib_p, 3)
    r_copy = sib(retb.at[away], sib_r, 4)
    sib(rows_a.at[away], rows_a.at[away], 1).wait_recv()
    sib(rows_c.at[away], rows_c.at[away], 2).wait_recv()
    loop(0, tiles, lambda i: expert_tile((1 - c) * tiles + i))
    p_copy.start()
    r_copy.start()
    loop(0, tiles, lambda i: expert_tile(c * tiles + i))
    v_copy = sib(vw.at[1 - c], sibvw, 5)
    v_copy.start()

    def pair_sum(i):
        at = pl.ds(pl.multiple_of(i * RT, RT), RT)
        mine = pl.ds(pl.multiple_of(c * SL + i * RT, RT), RT)
        prodb[mine, :] = (prodb[mine, :].astype(F32) + sib_p[at, :].astype(F32)).astype(BF16)

    def pair_sum_r(i):
        at = pl.ds(pl.multiple_of(i * RT, RT), RT)
        mine = pl.ds(pl.multiple_of(c * SL + i * RT, RT), RT)
        retb[mine, :] = (retb[mine, :].astype(F32) + sib_r[at, :].astype(F32)).astype(BF16)

    def give(a, src, dst, k):
        return remote(
            src.at[pl.ds(pl.multiple_of(c * SL + plane(k, 1) * CAP, CAP), CAP)],
            dst.at[pl.ds(pl.multiple_of(p * CAP, CAP), CAP)],
            xy_s.at[a, k],
            xy_q.at[a, k],
            plane_id(k),
        )

    mine_rows = pl.ds(pl.multiple_of(c * SL + p * CAP, CAP), CAP)
    here_rows = pl.ds(pl.multiple_of(p * CAP, CAP), CAP)
    r_copy.wait_recv()
    loop(0, tiles, pair_sum_r)
    loop(1, NP, lambda k: give(3, retb, got_r, k).start())
    got_r[here_rows, :] = retb[mine_rows, :]
    p_copy.wait_recv()
    loop(0, tiles, pair_sum)
    loop(1, NP, lambda k: give(2, prodb, got_p, k).start())
    got_p[here_rows, :] = prodb[mine_rows, :]

    v_copy.wait_recv()
    vz[z, :, :] = vw[c, :, :] + sibvw[...]

    def v_send(k):
        return remote(vz.at[z], vz.at[z], vz_s.at[0, k], vz_q.at[0, k], z_id(lax.rem(z + k, NZ)))

    def v_arrival(k):
        here = vz.at[lax.rem(z + NZ - k, NZ)]
        return remote(here, here, vz_s.at[0, k], vz_q.at[0, k], z_id(lax.rem(z + k, NZ)))

    loop(1, NZ, lambda k: v_send(k).start())

    def grads(i):
        at = pl.ds(pl.multiple_of(i * W, W), W)
        gout[:, at] = dot(ga_t[...], rows_c[:, at]).astype(BF16)
        gin[at, :] = jnp.transpose(dot(d_t[...], rows_a[:, at])).astype(BF16)

    loop(0, D // W, grads)

    loop(1, NZ, lambda k: v_arrival(k).wait_recv())
    vp[p, 0, :, :] = jnp.sum(vz[0:ZL], axis=0)
    vp[p, 1, :, :] = jnp.sum(vz[ZL:NZ], axis=0)

    def vp_send(k):
        return remote(vp.at[p], vp.at[p], vz_s.at[1, k], vz_q.at[1, k], plane_id(k))

    def vp_arrival(k):
        here = vp.at[plane(k, -1)]
        return remote(here, here, vz_s.at[1, k], vz_q.at[1, k], plane_id(k))

    loop(1, NP, lambda k: vp_send(k).start())

    def ring_copy(a, d, s):
        src = part.at[a, d, s]
        return remote(
            src, ring.at[a, d, s], rs_s.at[a, d, s], rs_q.at[a, d, s], right if d == 0 else left
        )

    def combine(a, got):
        def one(s):
            at = pl.ds(pl.multiple_of(s * W, W), W)
            value = dot(pcomb[...], got[:, at]).astype(BF16)
            part[a, 0, s, :, :] = value
            part[a, 1, s, :, :] = value

        loop(0, ZL, one)

    def ring_step(a, j, run):
        to_r = lax.rem(r + ZL - j, NZ)

        @pl.when(to_r < ZL)
        def _():
            s = lax.rem(to_r, ZL)
            if run:

                @pl.when(j >= 1)
                def _():
                    ring_copy(a, 0, s).wait_recv()
                    part[a, 0, s, :, :] = (
                        part[a, 0, s, :, :].astype(F32) + ring[a, 0, s, :, :].astype(F32)
                    ).astype(BF16)

                ring_copy(a, 0, s).start()
            else:
                ring_copy(a, 0, s).wait_send()

        to_l = lax.rem(r + NZ - ZL + 1 + j, NZ)

        @pl.when((to_l < ZL) & (j < ZL - 1))
        def _():
            s = lax.rem(to_l, ZL)
            if run:

                @pl.when(j >= 1)
                def _():
                    ring_copy(a, 1, s).wait_recv()
                    part[a, 1, s, :, :] = (
                        part[a, 1, s, :, :].astype(F32) + ring[a, 1, s, :, :].astype(F32)
                    ).astype(BF16)

                ring_copy(a, 1, s).start()
            else:
                ring_copy(a, 1, s).wait_send()

    loop(1, NP, lambda k: xy_arrival(3, got_r, 0, k).wait_recv())
    combine(1, got_r)
    extra = jnp.transpose(got_r[:, D : D + W].astype(F32)).astype(BF16)
    t0 = dot(extra, p0t[...])
    t1 = dot(extra, p1t[...])
    scal[z, 0:1, :] = t0[0:1, :]
    scal[z, 1:2, :] = t1[0:1, :]
    scal[z, 2:4, :] = t0[1:3, :] + t1[1:3, :]
    scal[z, 4:8, :] = jnp.zeros((4, T), F32)

    def sc_copy(s):
        to = lax.rem(s + ZL * c, NZ)
        return remote(scal.at[z], scal.at[z], sc_s.at[s], sc_q.at[z], z_id(to))

    def sc_arrival(k):
        here = scal.at[k]
        return remote(here, here, sc_s.at[0], sc_q.at[k], right)

    loop(0, ZL, lambda s: pl.when(s != r)(lambda: sc_copy(s).start()))
    ring_step(1, 0, True)
    loop(1, NP, lambda k: xy_arrival(2, got_p, 0, k).wait_recv())
    combine(0, got_p)
    ring_step(0, 0, True)

    def both(j):
        ring_step(1, j, True)
        ring_step(0, j, True)

    loop(1, ZL, both)

    loop(1, NP, lambda k: vp_arrival(k).wait_recv())
    vp_copy = sib(vp, vout.at[c], 6)
    vp_copy.start()
    vout[c, :, :, :, :] = vp[...]

    t_copy = sib(tail, tail, 7)

    @pl.when(own)
    def _():
        s = lax.rem(r, ZL)
        cols = pl.ds(pl.multiple_of(zl * W, W), W)
        router_all = routerT[...]
        router_h = router_all.astype(BF16)
        router_l = (router_all - router_h.astype(F32)).astype(BF16)
        logits = jnp.zeros((E, T), F32)
        for b in range(ZL):
            at = slice(b * W, (b + 1) * W)
            logits += dot(router_h[:, at], nb[b], NT) + dot(router_l[:, at], nb[b], NT)
        r0 = rt[0:1, :].astype(F32)
        r1 = rt[1:2, :].astype(F32)
        ids = lax.broadcasted_iota(jnp.int32, (E, T), 0).astype(F32)
        rg = jnp.sum(router_all * gain[...], axis=1, keepdims=True)

        def sc_wait(k):
            pl.when(k != z)(lambda: sc_arrival(k).wait_recv())

        loop(0, NZ, sc_wait)
        total = jnp.sum(scal[...], axis=0)
        dl = jnp.where(ids == r0, total[0:1, :], 0.0) + jnp.where(ids == r1, total[1:2, :], 0.0)
        dl = dl * (1.0 - jax.nn.sigmoid(logits))
        sum_1 = total[2:3, :] + jnp.sum(dl * rg, axis=0, keepdims=True)
        sum_2 = total[3:4, :] + jnp.sum(dl * logits, axis=0, keepdims=True)
        sum_1 = jnp.transpose(jnp.broadcast_to(sum_1, (W, T))) * (1.0 / D)
        sum_2 = jnp.transpose(jnp.broadcast_to(sum_2, (W, T))) * (1.0 / D)
        dl_c = jnp.transpose(jnp.concatenate([dl, jnp.zeros((W - E, T), F32)], axis=0))
        router_cols = jnp.concatenate([routerT[:, cols], jnp.zeros((W - E, W), F32)], axis=0)
        second = dot(dl_c.astype(BF16), router_cols.astype(BF16))
        values = frames[:, cols].astype(F32)
        inverse = stats[1]
        scaled = (values - stats[0]) * inverse

        def arrived_sum(a):
            ring_copy(a, 0, s).wait_recv()
            ring_copy(a, 1, s).wait_recv()
            return (
                part[a, 0, s, :, :].astype(F32)
                + ring[a, 0, s, :, :].astype(F32)
                + ring[a, 1, s, :, :].astype(F32)
            )

        d_scaled = (arrived_sum(1) + second) * gain[:, cols]
        result = cotb[s, :, :].astype(F32) + inverse * (d_scaled - sum_1 - scaled * sum_2)
        tail[1, :, :] = result.astype(BF16)
        tail[0, :, :] = (values + arrived_sum(0)).astype(BF16)
        t_copy.start()

    pl.when(jnp.logical_not(own))(lambda: t_copy.wait_recv())

    @pl.when(c == 0)
    def _():
        mixed[...] = tail[0, :, 0 : W // 2]
        dfr[...] = tail[1, :, 0 : W // 2]

    @pl.when(c == 1)
    def _():
        mixed[...] = tail[0, :, W // 2 : W]
        dfr[...] = tail[1, :, W // 2 : W]

    @pl.when(own)
    def _():
        t_copy.wait_send()
        rt_copy.wait_send()
        pl.when(r == ZL - 1)(lambda: loop(0, ZL, lambda s: nrm(s, right).wait_send()))
        pl.when(r == 0)(lambda: loop(0, ZL, lambda s: nrm(s, left).wait_send()))

    @pl.when(jnp.logical_not(own))
    def _():
        cot_copy.wait_send()
        pl.when(r < ZL + ZL // 2 - 1)(lambda: loop(0, ZL, lambda s: nrm(s, right).wait_send()))
        pl.when(r > ZL + ZL // 2)(lambda: loop(0, ZL, lambda s: nrm(s, left).wait_send()))

    loop(0, ZL + 1, lambda j: cot_step(j, False))

    def last_xy(k):
        xy(0, send_n, rows_a, c * SL, k).wait_send()
        xy(1, send_c, rows_c, c * SL, k).wait_send()
        give(3, retb, got_r, k).wait_send()
        give(2, prodb, got_p, k).wait_send()
        vp_send(k).wait_send()

    loop(1, NP, last_xy)
    loop(1, NZ, lambda k: v_send(k).wait_send())
    loop(0, ZL, lambda s: pl.when(s != r)(lambda: sc_copy(s).wait_send()))

    def last_ring(j):
        ring_step(0, j, False)
        ring_step(1, j, False)

    loop(0, ZL, last_ring)
    sib(vp, vout.at[1 - c], 6).wait_recv()
    for copy in (a_copy, c_copy, p_copy, r_copy, v_copy, vp_copy):
        copy.wait_send()


def shards(dims, frames, norm_gain, router, routes, w_in, w_out, cotangent):
    X, Y, ZL = dims
    NP, NZ, W = X * Y, 2 * ZL, 128
    T, D = frames.shape
    E = router.shape[1]
    CAP = 4 * routes.shape[1] * T // (3 * E)
    SL = NP * CAP
    HS = w_in.shape[2]
    vmem = pl.BlockSpec(memory_space=pltpu.VMEM)
    dma = pltpu.SemaphoreType.DMA
    mixed, dfr, sums, gin, gout = pl.pallas_call(
        functools.partial(kernel, dims),
        out_shape=[
            jax.ShapeDtypeStruct((T, W // 2), BF16),
            jax.ShapeDtypeStruct((T, W // 2), BF16),
            jax.ShapeDtypeStruct((2, NP, 2, D // W, W), F32),
            jax.ShapeDtypeStruct((D, HS), BF16),
            jax.ShapeDtypeStruct((HS, D), BF16),
        ],
        in_specs=[vmem] * 7,
        out_specs=[vmem] * 5,
        scratch_shapes=[
            pltpu.VMEM((8, T), jnp.int32),
            pltpu.VMEM((ZL, T, W), BF16),
            pltpu.VMEM((ZL, T, W), BF16),
            pltpu.VMEM((T, W // 2), BF16),
            pltpu.VMEM((2, T, W), F32),
            pltpu.VMEM((SL, T), BF16),
            pltpu.VMEM((SL, T), BF16),
            pltpu.VMEM((T, SL), BF16),
            pltpu.VMEM((SL, D), BF16),
            pltpu.VMEM((SL, D), BF16),
            pltpu.VMEM((2 * SL, D), BF16),
            pltpu.VMEM((2 * SL, D), BF16),
            pltpu.VMEM((HS, 2 * SL), BF16),
            pltpu.VMEM((HS, 2 * SL), BF16),
            pltpu.VMEM((2 * SL, D), BF16),
            pltpu.VMEM((2 * SL, D + W), BF16),
            pltpu.VMEM((SL, D), BF16),
            pltpu.VMEM((SL, D + W), BF16),
            pltpu.VMEM((SL, D), BF16),
            pltpu.VMEM((SL, D + W), BF16),
            pltpu.VMEM((2, 2, ZL, T, W), BF16),
            pltpu.VMEM((2, 2, ZL, T, W), BF16),
            pltpu.VMEM((NZ, 8, T), F32),
            pltpu.VMEM((2, D // W, W), F32),
            pltpu.VMEM((D // W, W), F32),
            pltpu.VMEM((NZ, D // W, W), F32),
            pltpu.VMEM((NP, 2, D // W, W), F32),
            pltpu.VMEM((2, T, W), BF16),
            dma((8,)),
            dma((8,)),
            dma((2,)),
            dma((ZL,)),
            dma((ZL,)),
            dma((ZL,)),
            dma((ZL,)),
            dma((ZL,)),
            dma((4, NP)),
            dma((4, NP)),
            dma((2, 2, ZL)),
            dma((2, 2, ZL)),
            dma((ZL,)),
            dma((NZ,)),
            dma((2, max(NP, NZ))),
            dma((2, max(NP, NZ))),
        ],
        compiler_params=pltpu.CompilerParams(
            collective_id=0, has_side_effects=True, vmem_limit_bytes=56 * 1024 * 1024
        ),
        name="experts",
    )(
        frames,
        norm_gain.reshape(1, D),
        router.T,
        jnp.pad(routes.T, ((0, 8 - routes.shape[1]), (0, 0))),
        w_in.reshape(D, HS),
        w_out.reshape(HS, D),
        cotangent,
    )
    column = lax.axis_index("expert")
    router_sum = sums[0].transpose(1, 0, 2, 3).reshape(E, D)
    d_router = router_sum.T * (1.0 / T)
    gain_sum = jnp.sum(sums[1, :, 0] + sums[1, :, 1], axis=0).reshape(D) * (1.0 / T)
    d_gain = (gain_sum + jnp.sum(router * d_router, axis=1)) / norm_gain
    d_gain = lax.dynamic_slice_in_dim(d_gain, column * (W // 2), W // 2, 0)
    return mixed, dfr, d_gain, d_router, gin.reshape(1, D, HS), gout.reshape(1, HS, D)


def plan(mesh):
    dp, ex = mesh.shape["dp"], mesh.shape["expert"]
    side = 4 if dp == 32 else 2
    return side, dp // 2 // side, ex // 2


def solution(mesh):
    placed = (
        P("dp", None),
        P(),
        P(),
        P("dp", None),
        P("dp", None, "expert"),
        P("dp", "expert", None),
        P("dp", "expert"),
    )
    return jax.shard_map(
        functools.partial(shards, plan(mesh)),
        mesh=mesh,
        in_specs=placed,
        out_specs=(
            P("dp", "expert"),
            P("dp", "expert"),
            P("expert"),
            P(),
            P("dp", None, "expert"),
            P("dp", "expert", None),
        ),
        check_vma=False,
    )
```

time: 1360 us -> 177 us (0.13)
  waiting for transfers between devices: 905 us -> 0 us
  blocking collectives: 338 us -> 0 us
  Pallas kernels: 0 us -> 166 us
  starting transfers between devices: 33.2 us -> 0 us
  local copies, waits for them, and re-layouts: 37.3 us -> 8.72 us
  matrix products: 15.7 us -> 0 us
  other arithmetic: 15.8 us -> 1.6 us
    psum x1 -> x0, waiting for transfers between devices: 528 us -> none  [shards(): lax.psum((jnp.sum(d_normed * scaled_cols, axis=0), jnp.dot(normed.astype(...]
    reduce_scatter x2 -> x0, waiting for transfers between devices: 262 us -> none  [the longest x1 146 us: shards(): lax.psum_scatter(partial_value.astype(jnp.bfloat16), 'expert', scatter_di...]
    psum x3 -> x0, blocking collectives: 245 us -> none  [the longest x1 135 us: shards(): lax.psum((jnp.sum(d_normed * scaled_cols, axis=0), jnp.dot(normed.astype(...]
    pallas_call x0 -> x1, Pallas kernels: none -> 166 us  [shards(): pl.pallas_call(functools.partial(kernel, dims), out_shape=[jax.ShapeDtype...]
    all_gather x1 -> x0, waiting for transfers between devices: 94.9 us -> none  [shards(): lax.all_gather(grads_cols.reshape(dp_size * capacity, col_width), 'expert...]
    all_to_all x2 -> x0, blocking collectives: 93.6 us -> none  [the longest x1 70.9 us: shards(): lax.all_to_all(sendbuf.reshape(experts, capacity, width_all), 'dp', split...]
    all_to_all x2 -> x0, starting transfers between devices: 32.9 us -> none  [the longest x1 16.5 us: shards(): lax.all_to_all(back_cols.reshape(dp_size, capacity, col_width), 'dp', spl...]
    all_to_all x2 -> x0, waiting for transfers between devices: 20.5 us -> none  [the longest x1 11.7 us: shards(): lax.all_to_all(back_cols.reshape(dp_size, capacity, col_width), 'dp', spl...]
  transfers between devices with their start and end apart: 6 -> 0, of which waited for: 6 -> 0; matrix products, arithmetic and copies ran while one was open for 2% -> 0% of each run, Pallas kernels for 0% -> 0%
where the time goes in v1:
time: 177 us
  Pallas kernels  166 us (94%)
  local copies, waits for them, and re-layouts  8.72 us (5%)
    pallas_call x1, Pallas kernels, shards(): pl.pallas_call(functools.partial(kernel, dims), out_shape=[jax.ShapeDtype...  166 us
    unnamed x19, local copies, waits for them, and re-layouts  7.51 us

profile of v1, /device:TPU:1, one launch (start us, length us, event | category | flops | bytes accessed | tf_op | source)
XLA Modules:
  0.0 177.1 jit_solution(7030887739344371599)
XLA Ops:
  0.6 0.0 copy-start.6
  0.6 0.7 copy-done.6
  1.3 0.6 pad.4.routesT
  1.9 1.5 copy.16.cot
  3.5 166.1 %experts.1 = (bf16[384,64]{1,0:T(8,128)(2,1)}, bf16[384,64]{1,0:T(8,128)(2,1)}, f32[2,16,2,8,128]{4,3,2,1,0:T(8,128)}, bf16[1024,256]{1,0:T(8,128)(2,1)}, bf16[256,1024]{1,0:T(8,128)(2,1)}) custom-call(bf16[384,1024]{1,0:T(8,128)(2,1)} %frames.1, f32[1,1024]{1,0:T(1,128)} %bitcast.29, f32[32,1024]{1,0:T(8,128)} %bitcast.23, s32[8,384]{1,0:T(8,128)} %pad.4.routesT, ...), custom_call_target="tpu_custom_call" | custom-call | tf_op jit(solution)/shard_map/experts/pallas_call | solution.py:622
  169.5 0.0 copy-start.3
  169.5 1.6 copy.18
  171.2 0.9 add_reduce_fusion
  172.1 0.0 copy-done.3
  172.1 0.0 copy-start.4
  172.1 0.0 copy-start
  172.1 0.0 copy-start.2
  172.2 0.9 copy-done
  173.1 0.0 copy-start.5
  173.1 0.7 multiply_reduce_fusion
  173.7 0.0 copy-done.5
  173.8 0.6 dynamic_slice.3
  174.3 0.0 copy-done.4
  174.3 0.7 copy.19
  175.1 0.0 copy-done.2
  175.1 0.0 copy-start.1
  175.1 0.8 copy.25
  175.9 0.4 copy-done.1
  176.3 0.8 copy.26
  (3 shorter events, 0.0 us)
Async XLA Ops:
  0.6 0.7 copy-start.6
  169.5 2.5 %copy-start.3 = (f32[2,16,2,8,128]{4,3,2,1,0:T(8,128)S(1)}, f32[2,16,2,8,128]{4,3,2,1,0:T(8,128)}, u32[]{:S(2)}) copy-start(f32[2,16,2,8,128]{4,3,2,1,0:T(8,128)} %get-tuple-element.13) | copy-start | bytes 786436
  172.1 2.3 %copy-start.4 = (bf16[384,64]{1,0:T(8,128)(2,1)S(1)}, bf16[384,64]{1,0:T(8,128)(2,1)}, u32[]{:S(2)}) copy-start(bf16[384,64]{1,0:T(8,128)(2,1)} %get-tuple-element.23) | copy-start | bytes 147460
  172.1 0.9 copy-start
  172.1 2.9 %copy-start.2 = (bf16[1024,256]{1,0:T(8,128)(2,1)S(1)}, bf16[1024,256]{1,0:T(8,128)(2,1)}, u32[]{:S(2)}) copy-start(bf16[1024,256]{1,0:T(8,128)(2,1)} %get-tuple-element.14) | copy-start | bytes 1572868
  173.1 0.7 copy-start.5
  175.1 1.2 copy-start.1

commit v2 on v1

--- a/solution.py
+++ b/solution.py
@@ -25,6 +25,10 @@
         return carry
 
     lax.fori_loop(lo, hi, step, 0)
+
+
+PARENT = {1: 0, 2: 0, 3: 2, 4: 0, 5: 4, 6: 4, 7: 6, 8: 6}
+LAST = {1: 0, 2: 1, 4: 2}
 
 
 def kernel(
@@ -53,6 +57,8 @@
     send_c,
     rows_a,
     rows_c,
+    hid,
+    gates,
     ga_t,
     d_t,
     prodb,
@@ -62,7 +68,8 @@
     got_p,
     got_r,
     part,
-    ring,
+    relay,
+    fin,
     scal,
     vw,
     sibvw,
@@ -74,13 +81,14 @@
     rt_sem,
     nrm_s,
     nrm_q,
-    cot_r,
-    cot_l,
+    cot_s0,
+    cot_s1,
     cot_q,
     xy_s,
     xy_q,
-    rs_s,
-    rs_q,
+    up_s,
+    relay_q,
+    fin_q,
     sc_s,
     sc_q,
     vz_s,
@@ -94,6 +102,7 @@
     CAP = SL // NP
     E = routerT.shape[0]
     W = 128
+    reach = (ZL, ZL - 1)
     dp = lax.axis_index("dp")
     ex = lax.axis_index("expert")
     p = lax.rem(dp, NP)
@@ -110,8 +119,11 @@
     def z_id(to):
         return ((to // ZL) * NP + p, lax.rem(to, ZL) * 2 + c)
 
-    right = z_id(lax.rem(z + 1, NZ))
-    left = z_id(lax.rem(z + NZ - 1, NZ))
+    def z_at(way, hops):
+        return z_id(lax.rem(z + (hops if way == 0 else NZ - hops), NZ))
+
+    right = z_at(0, 1)
+    left = z_at(1, 1)
 
     def plane(k, sign):
         px = lax.rem(x + X + sign * (k // Y), X)
@@ -165,35 +177,36 @@
     def nrm(s, to):
         return remote(nb.at[s], nb.at[s], nrm_s.at[s], nrm_q.at[s], to)
 
-    def cot_piece(s, sems, to):
-        return remote(cotb.at[s], cotb.at[s], sems.at[s], cot_q.at[s], to)
-
-    def cot_step(j, run):
-        piece = lax.rem(r + NZ - j, NZ)
-
-        @pl.when(piece < ZL)
-        def _():
-            s = lax.rem(piece, ZL)
-            if run:
-                pl.when(j >= 1)(lambda: cot_piece(s, cot_r, right).wait_recv())
-            pl.when(j < ZL)(
-                lambda: cot_piece(s, cot_r, right).start()
-                if run
-                else cot_piece(s, cot_r, right).wait_send()
-            )
-
-        other = lax.rem(r + j, NZ)
-
-        @pl.when((other < ZL) & (j < ZL))
-        def _():
-            s = lax.rem(other, ZL)
-            if run:
-                pl.when(j >= 1)(lambda: cot_piece(s, cot_l, left).wait_recv())
-            pl.when(j < ZL - 1)(
-                lambda: cot_piece(s, cot_l, left).start()
-                if run
-                else cot_piece(s, cot_l, left).wait_send()
-            )
+    def cot_copy_to(s, sem, way, hops):
+        return remote(cotb.at[s], cotb.at[s], sem, cot_q.at[s], z_at(way, hops))
+
+    def cot_source(act):
+        s = lax.rem(r, ZL)
+        for d in (4, 2, 1):
+            for way in (0, 1):
+                if d <= reach[way]:
+                    act(cot_copy_to(s, cot_s0.at[way * 3 + LAST[d]], way, d))
+
+    def cot_relay(d, act, wait=True):
+        for way in (0, 1):
+            if d > reach[way]:
+                continue
+            piece = lax.rem(r + (NZ - d if way == 0 else d), NZ)
+
+            @pl.when(piece < ZL)
+            def _():
+                s = lax.rem(piece, ZL)
+                if wait:
+                    cot_copy_to(s, cot_s1.at[s, 0], way, 1).wait_recv()
+                for far in (d + 2, d + 1):
+                    if far <= reach[way] and PARENT[far] == d:
+                        act(cot_copy_to(s, cot_s1.at[s, far - d - 1], way, far - d))
+
+    def start(copy):
+        copy.start()
+
+    def sent(copy):
+        copy.wait_send()
 
     def positions():
         r0 = rt[0:1, :].astype(F32)
@@ -260,10 +273,11 @@
         def _():
             cotb[r, :, :] = jnp.concatenate([two, one], axis=1)
 
-        cot_step(0, True)
+        cot_source(start)
         positions()
         dispatch(0, nb, send_n, rows_a)
-        loop(1, ZL + 1, lambda j: cot_step(j, True))
+        for d in (2, 4, 6):
+            cot_relay(d, start)
 
     @pl.when(jnp.logical_not(own))
     def _():
@@ -284,112 +298,130 @@
                 nrm(i, left).wait_recv()
                 pl.when(r > ZL + ZL // 2)(lambda: nrm(i, left).start())
 
-            cot_step(i + 1, True)
-
-        loop(0, ZL, step)
+        loop(0, ZL // 2, step)
+        cot_relay(2, start)
+        cot_relay(4, start)
+        loop(ZL // 2, ZL, step)
+        cot_relay(6, start)
         dispatch(0, nb, send_n, rows_a)
 
+    for d in (1, 3, 5, 7, 8):
+        cot_relay(d, start)
     dispatch(1, cotb, send_c, rows_c)
 
     half = pl.ds(pl.multiple_of(c * SL, SL), SL)
+    away = pl.ds(pl.multiple_of((1 - c) * SL, SL), SL)
+    RT = 128
+    tiles = SL // RT
+    mine_rows = pl.ds(pl.multiple_of(c * SL + p * CAP, CAP), CAP)
+    here_rows = pl.ds(pl.multiple_of(p * CAP, CAP), CAP)
+
     a_copy = sib(rows_a.at[half], rows_a.at[half], 1)
-    c_copy = sib(rows_c.at[half], rows_c.at[half], 2)
     loop(1, NP, lambda k: xy_arrival(0, rows_a, c * SL, k).wait_recv())
     a_copy.start()
-    loop(1, NP, lambda k: xy_arrival(1, rows_c, c * SL, k).wait_recv())
-    c_copy.start()
-
-    gain_hi = gain[...].astype(BF16)
-    gain_lo = (gain[...] - gain_hi.astype(F32)).astype(BF16)
     weight_in = w_in[...]
     weight_out = w_out[...]
-    gw = (
-        dot(jnp.broadcast_to(gain_hi, (16, D)), weight_in)
-        + dot(jnp.broadcast_to(gain_lo, (16, D)), weight_in)
-    )[0:1, :]
     router_row = routerT[pl.ds(dp, 1), :]
     router_hi = router_row.astype(BF16)
     router_lo = (router_row - router_hi.astype(F32)).astype(BF16)
     router_hi = jnp.broadcast_to(router_hi, (16, D))
     router_lo = jnp.broadcast_to(router_lo, (16, D))
-    vw[...] = jnp.zeros_like(vw)
-    RT = 128
-    lane = lax.broadcasted_iota(jnp.int32, (RT, W), 1)
-
-    def expert_tile(i):
+
+    def forward(i):
         at = pl.ds(pl.multiple_of(i * RT, RT), RT)
         arrived = rows_a[at, :]
-        cots = rows_c[at, :]
         hidden = dot(arrived, weight_in)
         logit = dot(arrived, router_hi, NT) + dot(arrived, router_lo, NT)
         gate = jax.nn.sigmoid(logit[:, 0:1])
+        active = hidden * jax.nn.sigmoid(hidden)
+        ga = active.astype(BF16).astype(F32) * (0.5 * gate)
+        hid[at, :] = hidden
+        gates[at, :] = jnp.broadcast_to(gate, (RT, W))
+        ga_t[:, at] = jnp.transpose(ga).astype(BF16)
+        prodb[at, :] = dot(ga.astype(BF16), weight_out).astype(BF16)
+
+    def pair_sum(buf, other, i):
+        at = pl.ds(pl.multiple_of(i * RT, RT), RT)
+        mine = pl.ds(pl.multiple_of(c * SL + i * RT, RT), RT)
+        buf[mine, :] = (buf[mine, :].astype(F32) + other[at, :].astype(F32)).astype(BF16)
+
+    def give(a, h, src, dst, k):
+        wide = src.shape[1]
+        cut = wide - D // 2
+        cols = pl.ds(0, cut) if h == 0 else pl.ds(cut, D // 2)
+        return remote(
+            src.at[pl.ds(pl.multiple_of(c * SL + plane(k, 1) * CAP, CAP), CAP), cols],
+            dst.at[here_rows, cols],
+            xy_s.at[2 + 2 * a + h, k],
+            xy_q.at[2 + 2 * a + h, k],
+            plane_id(k),
+        )
+
+    def give_arrival(a, h, dst, k):
+        wide = dst.shape[1]
+        cut = wide - D // 2
+        cols = pl.ds(0, cut) if h == 0 else pl.ds(cut, D // 2)
+        here = dst.at[pl.ds(pl.multiple_of(plane(k, -1) * CAP, CAP), CAP), cols]
+        return remote(here, here, xy_s.at[2 + 2 * a + h, k], xy_q.at[2 + 2 * a + h, k], plane_id(k))
+
+    p_copy = sib(prodb.at[away], sib_p, 3)
+    sib(rows_a.at[away], rows_a.at[away], 1).wait_recv()
+    loop(0, tiles, lambda i: forward((1 - c) * tiles + i))
+    p_copy.start()
+    loop(0, tiles, lambda i: forward(c * tiles + i))
+    p_copy.wait_recv()
+    loop(0, tiles, lambda i: pair_sum(prodb, sib_p, i))
+    for h in (0, 1):
+        loop(1, NP, lambda k: give(0, h, prodb, got_p, k).start())
+    got_p[here_rows, :] = prodb[mine_rows, :]
+
+    c_copy = sib(rows_c.at[half], rows_c.at[half], 2)
+    loop(1, NP, lambda k: xy_arrival(1, rows_c, c * SL, k).wait_recv())
+    c_copy.start()
+    gain_hi = gain[...].astype(BF16)
+    gain_lo = (gain[...] - gain_hi.astype(F32)).astype(BF16)
+    gw = (
+        dot(jnp.broadcast_to(gain_hi, (16, D)), weight_in)
+        + dot(jnp.broadcast_to(gain_lo, (16, D)), weight_in)
+    )[0:1, :]
+    vw[...] = jnp.zeros_like(vw)
+    lane = lax.broadcasted_iota(jnp.int32, (RT, W), 1)
+
+    def backward(i):
+        at = pl.ds(pl.multiple_of(i * RT, RT), RT)
+        hidden = hid[at, :]
+        gate = gates[at, 0:1]
         sig = jax.nn.sigmoid(hidden)
-        active = hidden * sig
-        up = dot(cots, weight_out, NT) * (0.5 * gate)
-        ga = active.astype(BF16).astype(F32) * (0.5 * gate)
+        up = dot(rows_c[at, :], weight_out, NT) * (0.5 * gate)
         dh = up * (sig * (1.0 + hidden * (1.0 - sig)))
-        dh_b = dh.astype(BF16)
-        ga_b = ga.astype(BF16)
-        ga_t[:, at] = jnp.transpose(ga).astype(BF16)
         d_t[:, at] = jnp.transpose(dh).astype(BF16)
-        dgg = jnp.sum(up * active, axis=1, keepdims=True)
+        dgg = jnp.sum(up * (hidden * sig), axis=1, keepdims=True)
         s1 = jnp.sum(dh * gw, axis=1, keepdims=True)
         s2 = jnp.sum(dh * hidden, axis=1, keepdims=True)
-        prodb[at, :] = dot(ga_b, weight_out).astype(BF16)
-        back = dot(dh_b, weight_in, NT)
-        retb[at, 0:D] = back.astype(BF16)
-        retb[at, D : D + W] = jnp.where(
+        back = dot(dh.astype(BF16), weight_in, NT)
+        retb[at, W : W + D] = back.astype(BF16)
+        retb[at, 0:W] = jnp.where(
             lane == 0, dgg, jnp.where(lane == 1, s1, jnp.where(lane == 2, s2, 0.0))
         ).astype(BF16)
-        wide = arrived.astype(F32)
+        wide = rows_a[at, :].astype(F32)
         v = jnp.sum(wide * (dgg * (1.0 - gate)), axis=0, keepdims=True)
         w = jnp.sum(wide * back, axis=0, keepdims=True)
         for b in range(D // W):
             vw[0, b : b + 1, :] += v[:, b * W : (b + 1) * W]
             vw[1, b : b + 1, :] += w[:, b * W : (b + 1) * W]
 
-    tiles = SL // RT
-    away = pl.ds(pl.multiple_of((1 - c) * SL, SL), SL)
-    p_copy = sib(prodb.at[away], sib_p, 3)
     r_copy = sib(retb.at[away], sib_r, 4)
-    sib(rows_a.at[away], rows_a.at[away], 1).wait_recv()
     sib(rows_c.at[away], rows_c.at[away], 2).wait_recv()
-    loop(0, tiles, lambda i: expert_tile((1 - c) * tiles + i))
-    p_copy.start()
+    loop(0, tiles, lambda i: backward((1 - c) * tiles + i))
     r_copy.start()
-    loop(0, tiles, lambda i: expert_tile(c * tiles + i))
+    loop(0, tiles, lambda i: backward(c * tiles + i))
     v_copy = sib(vw.at[1 - c], sibvw, 5)
     v_copy.start()
-
-    def pair_sum(i):
-        at = pl.ds(pl.multiple_of(i * RT, RT), RT)
-        mine = pl.ds(pl.multiple_of(c * SL + i * RT, RT), RT)
-        prodb[mine, :] = (prodb[mine, :].astype(F32) + sib_p[at, :].astype(F32)).astype(BF16)
-
-    def pair_sum_r(i):
-        at = pl.ds(pl.multiple_of(i * RT, RT), RT)
-        mine = pl.ds(pl.multiple_of(c * SL + i * RT, RT), RT)
-        retb[mine, :] = (retb[mine, :].astype(F32) + sib_r[at, :].astype(F32)).astype(BF16)
-
-    def give(a, src, dst, k):
-        return remote(
-            src.at[pl.ds(pl.multiple_of(c * SL + plane(k, 1) * CAP, CAP), CAP)],
-            dst.at[pl.ds(pl.multiple_of(p * CAP, CAP), CAP)],
-            xy_s.at[a, k],
-            xy_q.at[a, k],
-            plane_id(k),
-        )
-
-    mine_rows = pl.ds(pl.multiple_of(c * SL + p * CAP, CAP), CAP)
-    here_rows = pl.ds(pl.multiple_of(p * CAP, CAP), CAP)
     r_copy.wait_recv()
-    loop(0, tiles, pair_sum_r)
-    loop(1, NP, lambda k: give(3, retb, got_r, k).start())
+    loop(0, tiles, lambda i: pair_sum(retb, sib_r, i))
+    for h in (0, 1):
+        loop(1, NP, lambda k: give(1, h, retb, got_r, k).start())
     got_r[here_rows, :] = retb[mine_rows, :]
-    p_copy.wait_recv()
-    loop(0, tiles, pair_sum)
-    loop(1, NP, lambda k: give(2, prodb, got_p, k).start())
-    got_p[here_rows, :] = prodb[mine_rows, :]
 
     v_copy.wait_recv()
     vz[z, :, :] = vw[c, :, :] + sibvw[...]
@@ -402,13 +434,65 @@
         return remote(here, here, vz_s.at[0, k], vz_q.at[0, k], z_id(lax.rem(z + k, NZ)))
 
     loop(1, NZ, lambda k: v_send(k).start())
+
+    def up(a, d, lo, hi, act, run=True):
+        for way in (0, 1):
+            if d > reach[way]:
+                continue
+            to = lax.rem(r + (d if way == 0 else NZ - d), NZ)
+
+            @pl.when((to >= lo) & (to < hi))
+            def _():
+                s = lax.rem(to, ZL)
+                pd = PARENT[d]
+                if pd == 0:
+                    dst, sem = fin.at[a, way * 3 + LAST[d]], fin_q.at[a, way * 3 + LAST[d]]
+                else:
+                    dst, sem = relay.at[a, s, 1 - d % 2], relay_q.at[a, s, 1 - d % 2]
+                if run:
+                    kids = [k for k in (d + 1, d + 2) if k <= reach[way] and PARENT[k] == d]
+                    total = None
+                    for kid in kids:
+                        q = 1 - kid % 2
+                        landed = relay.at[a, s, q]
+                        remote(landed, landed, up_s.at[a, s], relay_q.at[a, s, q], right).wait_recv()
+                        if total is None:
+                            total = part[a, s, :, :].astype(F32)
+                        total = total + relay[a, s, q, :, :].astype(F32)
+                    if kids:
+                        part[a, s, :, :] = total.astype(BF16)
+                act(remote(part.at[a, s], dst, up_s.at[a, s], sem, z_at(way, d - pd)))
+
+    def combine(a, h, got):
+        first = h * (ZL // 2)
+        off = got.shape[1] - D
+
+        def one(i):
+            s = first + i
+            at = pl.ds(pl.multiple_of(off + s * W, W), W)
+            part[a, s, :, :] = dot(pcomb[...], got[:, at]).astype(BF16)
+
+        loop(1, NP, lambda k: give_arrival(a, h, got, k).wait_recv())
+        loop(0, ZL // 2, one)
+        for d in (7, 8, 5, 3, 1):
+            up(a, d, first, first + ZL // 2, start)
+
+    def relays(a, ds, lo, hi):
+        for d in ds:
+            up(a, d, lo, hi, start)
+
+    combine(0, 0, got_p)
+    combine(0, 1, got_p)
 
     def grads(i):
         at = pl.ds(pl.multiple_of(i * W, W), W)
         gout[:, at] = dot(ga_t[...], rows_c[:, at]).astype(BF16)
         gin[at, :] = jnp.transpose(dot(d_t[...], rows_a[:, at])).astype(BF16)
 
-    loop(0, D // W, grads)
+    loop(0, D // W // 2, grads)
+    relays(0, (6, 2), 0, ZL)
+    loop(D // W // 2, D // W, grads)
+    relays(0, (4,), 0, ZL)
 
     loop(1, NZ, lambda k: v_arrival(k).wait_recv())
     vp[p, 0, :, :] = jnp.sum(vz[0:ZL], axis=0)
@@ -423,61 +507,8 @@
 
     loop(1, NP, lambda k: vp_send(k).start())
 
-    def ring_copy(a, d, s):
-        src = part.at[a, d, s]
-        return remote(
-            src, ring.at[a, d, s], rs_s.at[a, d, s], rs_q.at[a, d, s], right if d == 0 else left
-        )
-
-    def combine(a, got):
-        def one(s):
-            at = pl.ds(pl.multiple_of(s * W, W), W)
-            value = dot(pcomb[...], got[:, at]).astype(BF16)
-            part[a, 0, s, :, :] = value
-            part[a, 1, s, :, :] = value
-
-        loop(0, ZL, one)
-
-    def ring_step(a, j, run):
-        to_r = lax.rem(r + ZL - j, NZ)
-
-        @pl.when(to_r < ZL)
-        def _():
-            s = lax.rem(to_r, ZL)
-            if run:
-
-                @pl.when(j >= 1)
-                def _():
-                    ring_copy(a, 0, s).wait_recv()
-                    part[a, 0, s, :, :] = (
-                        part[a, 0, s, :, :].astype(F32) + ring[a, 0, s, :, :].astype(F32)
-                    ).astype(BF16)
-
-                ring_copy(a, 0, s).start()
-            else:
-                ring_copy(a, 0, s).wait_send()
-
-        to_l = lax.rem(r + NZ - ZL + 1 + j, NZ)
-
-        @pl.when((to_l < ZL) & (j < ZL - 1))
-        def _():
-            s = lax.rem(to_l, ZL)
-            if run:
-
-                @pl.when(j >= 1)
-                def _():
-                    ring_copy(a, 1, s).wait_recv()
-                    part[a, 1, s, :, :] = (
-                        part[a, 1, s, :, :].astype(F32) + ring[a, 1, s, :, :].astype(F32)
-                    ).astype(BF16)
-
-                ring_copy(a, 1, s).start()
-            else:
-                ring_copy(a, 1, s).wait_send()
-
-    loop(1, NP, lambda k: xy_arrival(3, got_r, 0, k).wait_recv())
-    combine(1, got_r)
-    extra = jnp.transpose(got_r[:, D : D + W].astype(F32)).astype(BF16)
+    combine(1, 0, got_r)
+    extra = jnp.transpose(got_r[:, 0:W].astype(F32)).astype(BF16)
     t0 = dot(extra, p0t[...])
     t1 = dot(extra, p1t[...])
     scal[z, 0:1, :] = t0[0:1, :]
@@ -494,16 +525,10 @@
         return remote(here, here, sc_s.at[0], sc_q.at[k], right)
 
     loop(0, ZL, lambda s: pl.when(s != r)(lambda: sc_copy(s).start()))
-    ring_step(1, 0, True)
-    loop(1, NP, lambda k: xy_arrival(2, got_p, 0, k).wait_recv())
-    combine(0, got_p)
-    ring_step(0, 0, True)
-
-    def both(j):
-        ring_step(1, j, True)
-        ring_step(0, j, True)
-
-    loop(1, ZL, both)
+    relays(1, (6, 2), 0, ZL // 2)
+    combine(1, 1, got_r)
+    relays(1, (4,), 0, ZL // 2)
+    relays(1, (6, 2, 4), ZL // 2, ZL)
 
     loop(1, NP, lambda k: vp_arrival(k).wait_recv())
     vp_copy = sib(vp, vout.at[c], 6)
@@ -547,18 +572,20 @@
         scaled = (values - stats[0]) * inverse
 
         def arrived_sum(a):
-            ring_copy(a, 0, s).wait_recv()
-            ring_copy(a, 1, s).wait_recv()
-            return (
-                part[a, 0, s, :, :].astype(F32)
-                + ring[a, 0, s, :, :].astype(F32)
-                + ring[a, 1, s, :, :].astype(F32)
-            )
-
+            total = part[a, s, :, :].astype(F32)
+            for way in (0, 1):
+                for d in (1, 2, 4):
+                    if d <= reach[way]:
+                        q = way * 3 + LAST[d]
+                        landed = fin.at[a, q]
+                        remote(landed, landed, up_s.at[a, s], fin_q.at[a, q], right).wait_recv()
+                        total = total + fin[a, q, :, :].astype(F32)
+            return total
+
+        tail[0, :, :] = (values + arrived_sum(0)).astype(BF16)
         d_scaled = (arrived_sum(1) + second) * gain[:, cols]
         result = cotb[s, :, :].astype(F32) + inverse * (d_scaled - sum_1 - scaled * sum_2)
         tail[1, :, :] = result.astype(BF16)
-        tail[0, :, :] = (values + arrived_sum(0)).astype(BF16)
         t_copy.start()
 
     pl.when(jnp.logical_not(own))(lambda: t_copy.wait_recv())
@@ -579,6 +606,7 @@
         rt_copy.wait_send()
         pl.when(r == ZL - 1)(lambda: loop(0, ZL, lambda s: nrm(s, right).wait_send()))
         pl.when(r == 0)(lambda: loop(0, ZL, lambda s: nrm(s, left).wait_send()))
+        cot_source(sent)
 
     @pl.when(jnp.logical_not(own))
     def _():
@@ -586,24 +614,23 @@
         pl.when(r < ZL + ZL // 2 - 1)(lambda: loop(0, ZL, lambda s: nrm(s, right).wait_send()))
         pl.when(r > ZL + ZL // 2)(lambda: loop(0, ZL, lambda s: nrm(s, left).wait_send()))
 
-    loop(0, ZL + 1, lambda j: cot_step(j, False))
+    for d in (2, 4, 6):
+        cot_relay(d, sent, wait=False)
 
     def last_xy(k):
         xy(0, send_n, rows_a, c * SL, k).wait_send()
         xy(1, send_c, rows_c, c * SL, k).wait_send()
-        give(3, retb, got_r, k).wait_send()
-        give(2, prodb, got_p, k).wait_send()
+        for h in (0, 1):
+            give(0, h, prodb, got_p, k).wait_send()
+            give(1, h, retb, got_r, k).wait_send()
         vp_send(k).wait_send()
 
     loop(1, NP, last_xy)
     loop(1, NZ, lambda k: v_send(k).wait_send())
     loop(0, ZL, lambda s: pl.when(s != r)(lambda: sc_copy(s).wait_send()))
-
-    def last_ring(j):
-        ring_step(0, j, False)
-        ring_step(1, j, False)
-
-    loop(0, ZL, last_ring)
+    for d in range(1, ZL + 1):
+        for a in (0, 1):
+            up(a, d, 0, ZL, sent, run=False)
     sib(vp, vout.at[1 - c], 6).wait_recv()
     for copy in (a_copy, c_copy, p_copy, r_copy, v_copy, vp_copy):
         copy.wait_send()
@@ -643,6 +670,8 @@
             pltpu.VMEM((SL, D), BF16),
             pltpu.VMEM((2 * SL, D), BF16),
             pltpu.VMEM((2 * SL, D), BF16),
+            pltpu.VMEM((2 * SL, HS), F32),
+            pltpu.VMEM((2 * SL, W), F32),
             pltpu.VMEM((HS, 2 * SL), BF16),
             pltpu.VMEM((HS, 2 * SL), BF16),
             pltpu.VMEM((2 * SL, D), BF16),
@@ -651,8 +680,9 @@
             pltpu.VMEM((SL, D + W), BF16),
             pltpu.VMEM((SL, D), BF16),
             pltpu.VMEM((SL, D + W), BF16),
-            pltpu.VMEM((2, 2, ZL, T, W), BF16),
-            pltpu.VMEM((2, 2, ZL, T, W), BF16),
+            pltpu.VMEM((2, ZL, T, W), BF16),
+            pltpu.VMEM((2, ZL, 2, T, W), BF16),
+            pltpu.VMEM((2, 6, T, W), BF16),
             pltpu.VMEM((NZ, 8, T), F32),
             pltpu.VMEM((2, D // W, W), F32),
             pltpu.VMEM((D // W, W), F32),
@@ -664,13 +694,14 @@
             dma((2,)),
             dma((ZL,)),
             dma((ZL,)),
+            dma((6,)),
+            dma((ZL, 2)),
             dma((ZL,)),
-            dma((ZL,)),
-            dma((ZL,)),
-            dma((4, NP)),
-            dma((4, NP)),
-            dma((2, 2, ZL)),
-            dma((2, 2, ZL)),
+            dma((6, NP)),
+            dma((6, NP)),
+            dma((2, ZL)),
+            dma((2, ZL, 2)),
+            dma((2, 6)),
             dma((ZL,)),
             dma((NZ,)),
             dma((2, max(NP, NZ))),

time: 177 us -> 149 us (0.84)
  Pallas kernels: 166 us -> 137 us
    pallas_call x1, Pallas kernels: 166 us -> 137 us  [shards(): pl.pallas_call(functools.partial(kernel, dims), out_shape=[jax.ShapeDtype...]
where the time goes in v2:
time: 149 us; the launch traced here: 148 us
  Pallas kernels  137 us (92%)
  local copies, waits for them, and re-layouts  8.72 us (6%)
  other arithmetic  1.6 us (1%)
    pallas_call x1, Pallas kernels, shards(): pl.pallas_call(functools.partial(kernel, dims), out_shape=[jax.ShapeDtype...  137 us
    unnamed x19, local copies, waits for them, and re-layouts  7.51 us

profile of v2, /device:TPU:1, one launch (start us, length us, event | category | flops | bytes accessed | tf_op | source)
XLA Modules:
  0.0 147.9 jit_solution(15931122177065276272)
XLA Ops:
  0.6 0.0 copy-start.6
  0.6 0.7 copy-done.6
  1.3 0.6 pad.4.routesT
  1.9 1.5 %copy.16.cot = bf16[384,64]{1,0:T(8,128)(2,1)} copy(bf16[384,64]{0,1:T(8,128)(2,1)} %param.13) | data formatting | bytes 98304 | tf_op args[6]
  3.5 136.9 %experts.1 = (bf16[384,64]{1,0:T(8,128)(2,1)}, bf16[384,64]{1,0:T(8,128)(2,1)}, f32[2,16,2,8,128]{4,3,2,1,0:T(8,128)}, bf16[1024,256]{1,0:T(8,128)(2,1)}, bf16[256,1024]{1,0:T(8,128)(2,1)}) custom-call(bf16[384,1024]{1,0:T(8,128)(2,1)} %frames.1, f32[1,1024]{1,0:T(1,128)} %bitcast.29, f32[32,1024]{1,0:T(8,128)} %bitcast.23, s32[8,384]{1,0:T(8,128)} %pad.4.routesT, ...), custom_call_target="tpu_custom_call" | custom-call | tf_op jit(solution)/shard_map/experts/pallas_call | solution.py:649
  140.3 0.0 copy-start.3
  140.3 1.6 %copy.18 = bf16[384,64]{0,1:T(8,128)(2,1)} copy(bf16[384,64]{1,0:T(8,128)(2,1)} %get-tuple-element.22) | data formatting | bytes 98304
  142.0 0.9 add_reduce_fusion
  142.9 0.0 copy-done.3
  142.9 0.0 copy-start.4
  142.9 0.0 copy-start
  142.9 0.0 copy-start.2
  143.0 0.9 copy-done
  143.9 0.0 copy-start.5
  143.9 0.7 multiply_reduce_fusion
  144.5 0.0 copy-done.5
  144.6 0.6 dynamic_slice.3
  145.1 0.0 copy-done.4
  145.1 0.7 copy.19
  145.9 0.0 copy-done.2
  145.9 0.0 copy-start.1
  145.9 0.8 copy.25
  146.7 0.4 copy-done.1
  147.1 0.8 copy.26
  (3 shorter events, 0.0 us)
Async XLA Ops:
  0.6 0.7 copy-start.6
  140.3 2.5 %copy-start.3 = (f32[2,16,2,8,128]{4,3,2,1,0:T(8,128)S(1)}, f32[2,16,2,8,128]{4,3,2,1,0:T(8,128)}, u32[]{:S(2)}) copy-start(f32[2,16,2,8,128]{4,3,2,1,0:T(8,128)} %get-tuple-element.13) | copy-start | bytes 786436
  142.9 2.3 %copy-start.4 = (bf16[384,64]{1,0:T(8,128)(2,1)S(1)}, bf16[384,64]{1,0:T(8,128)(2,1)}, u32[]{:S(2)}) copy-start(bf16[384,64]{1,0:T(8,128)(2,1)} %get-tuple-element.23) | copy-start | bytes 147460
  142.9 0.9 copy-start
  142.9 2.9 %copy-start.2 = (bf16[1024,256]{1,0:T(8,128)(2,1)S(1)}, bf16[1024,256]{1,0:T(8,128)(2,1)}, u32[]{:S(2)}) copy-start(bf16[1024,256]{1,0:T(8,128)(2,1)} %get-tuple-element.14) | copy-start | bytes 1572868
  143.9 0.7 copy-start.5
  145.9 1.2 copy-start.1

commit v3 on v2

--- a/solution.py
+++ b/solution.py
@@ -71,6 +71,7 @@
     relay,
     fin,
     scal,
+    logits_t,
     vw,
     sibvw,
     vz,
@@ -81,6 +82,7 @@
     rt_sem,
     nrm_s,
     nrm_q,
+    chain_s,
     cot_s0,
     cot_s1,
     cot_q,
@@ -177,36 +179,53 @@
     def nrm(s, to):
         return remote(nb.at[s], nb.at[s], nrm_s.at[s], nrm_q.at[s], to)
 
+    def pass_on(s, to):
+        return remote(cotb.at[s], cotb.at[s], chain_s.at[s], cot_q.at[s], to)
+
     def cot_copy_to(s, sem, way, hops):
         return remote(cotb.at[s], cotb.at[s], sem, cot_q.at[s], z_at(way, hops))
+
+    def inside(way, hops):
+        return (r + hops < ZL) if way == 0 else (r >= hops)
+
+    def to_other_block(s, act):
+        pl.when(r == ZL - 1)(lambda: act(pass_on(s, right)))
+        pl.when(r == 0)(lambda: act(pass_on(s, left)))
 
     def cot_source(act):
         s = lax.rem(r, ZL)
         for d in (4, 2, 1):
             for way in (0, 1):
-                if d <= reach[way]:
-                    act(cot_copy_to(s, cot_s0.at[way * 3 + LAST[d]], way, d))
+                copy = cot_copy_to(s, cot_s0.at[way * 3 + LAST[d]], way, d)
+                pl.when(inside(way, d))(functools.partial(act, copy))
+        to_other_block(s, act)
 
     def cot_relay(d, act, wait=True):
         for way in (0, 1):
-            if d > reach[way]:
-                continue
-            piece = lax.rem(r + (NZ - d if way == 0 else d), NZ)
-
-            @pl.when(piece < ZL)
+
+            @pl.when(inside(1 - way, d))
             def _():
-                s = lax.rem(piece, ZL)
+                s = lax.rem(r + (NZ - d if way == 0 else d), NZ)
                 if wait:
                     cot_copy_to(s, cot_s1.at[s, 0], way, 1).wait_recv()
                 for far in (d + 2, d + 1):
-                    if far <= reach[way] and PARENT[far] == d:
-                        act(cot_copy_to(s, cot_s1.at[s, far - d - 1], way, far - d))
+                    if far < ZL and PARENT[far] == d:
+                        copy = cot_copy_to(s, cot_s1.at[s, far - d - 1], way, far - d)
+                        pl.when(inside(way, far - d))(functools.partial(act, copy))
+                if way == 0:
+                    pl.when(r == ZL - 1)(lambda: act(pass_on(s, right)))
+                else:
+                    pl.when(r == 0)(lambda: act(pass_on(s, left)))
 
     def start(copy):
         copy.start()
 
     def sent(copy):
         copy.wait_send()
+
+    near = r < ZL + ZL // 2
+    onward_r = near & (r >= ZL) & (r < ZL + ZL // 2 - 1)
+    onward_l = r > ZL + ZL // 2
 
     def positions():
         r0 = rt[0:1, :].astype(F32)
@@ -233,34 +252,43 @@
                 else:
                     pcomb[:, b * W : (b + 1) * W] += hit
 
-    def xy(a, src, dst, at, k):
+    def half_cols(h):
+        return pl.ds(pl.multiple_of(h * (D // 2), D // 2), D // 2)
+
+    def xy(a, h, src, dst, k):
         return remote(
-            src.at[pl.ds(pl.multiple_of(plane(k, 1) * CAP, CAP), CAP)],
-            dst.at[pl.ds(pl.multiple_of(at + p * CAP, CAP), CAP)],
-            xy_s.at[a, k],
-            xy_q.at[a, k],
+            src.at[pl.ds(pl.multiple_of(plane(k, 1) * CAP, CAP), CAP), half_cols(h)],
+            dst.at[pl.ds(pl.multiple_of(c * SL + p * CAP, CAP), CAP), half_cols(h)],
+            xy_s.at[2 * a + h, k],
+            xy_q.at[2 * a + h, k],
             plane_id(k),
         )
 
-    def xy_arrival(a, dst, at, k):
-        here = dst.at[pl.ds(pl.multiple_of(at + plane(k, -1) * CAP, CAP), CAP)]
-        return remote(here, here, xy_s.at[a, k], xy_q.at[a, k], plane_id(k))
-
-    def dispatch(a, pieces, send, dst):
+    def xy_arrival(a, h, dst, k):
+        here = dst.at[
+            pl.ds(pl.multiple_of(c * SL + plane(k, -1) * CAP, CAP), CAP), half_cols(h)
+        ]
+        return remote(here, here, xy_s.at[2 * a + h, k], xy_q.at[2 * a + h, k], plane_id(k))
+
+    def to_slots(pieces, send, s):
         pt = p0t[...] + p1t[...]
-
-        def one(s):
-            send[:, pl.ds(pl.multiple_of(s * W, W), W)] = dot(pt, pieces[s]).astype(BF16)
-
-        loop(0, ZL, one)
-        loop(1, NP, lambda k: xy(a, send, dst, c * SL, k).start())
+        send[:, pl.ds(pl.multiple_of(s * W, W), W)] = dot(pt, pieces[s]).astype(BF16)
+
+    def go(a, h, send, dst):
+        loop(1, NP, lambda k: xy(a, h, send, dst, k).start())
+
+    def keep(send, dst):
         mine = pl.ds(pl.multiple_of(p * CAP, CAP), CAP)
         dst[pl.ds(pl.multiple_of(c * SL + p * CAP, CAP), CAP), :] = send[mine, :]
+
+    order = [d for d in (1, 2, 4, 3, 6, 5, 7) if d < ZL]
+    chain_order = [0] + order
+    enough = max(chain_order.index(d) for d in range(ZL // 2))
 
     @pl.when(own)
     def _():
         rt_copy.start()
-        pl.when(r == ZL - 1)(lambda: loop(0, ZL, lambda s: nrm(s, right).start()))
+        pl.when(r == ZL - 1)(lambda: loop(0, ZL, lambda i: nrm(ZL - 1 - i, right).start()))
         pl.when(r == 0)(lambda: loop(0, ZL, lambda s: nrm(s, left).start()))
         cot_copy.wait_recv()
         one, two = cot[...], sibcot[...]
@@ -275,39 +303,41 @@
 
         cot_source(start)
         positions()
-        dispatch(0, nb, send_n, rows_a)
-        for d in (2, 4, 6):
+        for h in (0, 1):
+            loop(h * (ZL // 2), (h + 1) * (ZL // 2), lambda s: to_slots(nb, send_n, s))
+            go(0, h, send_n, rows_a)
+        for d in order:
             cot_relay(d, start)
+        for h in (0, 1):
+            loop(h * (ZL // 2), (h + 1) * (ZL // 2), lambda s: to_slots(cotb, send_c, s))
+            go(1, h, send_c, rows_c)
 
     @pl.when(jnp.logical_not(own))
     def _():
         cot_copy.start()
         rt_copy.wait_recv()
         positions()
-
-        def step(i):
-            near = r < ZL + ZL // 2
-
-            @pl.when(near)
-            def _():
-                nrm(i, right).wait_recv()
-                pl.when(r < ZL + ZL // 2 - 1)(lambda: nrm(i, right).start())
-
-            @pl.when(jnp.logical_not(near))
-            def _():
-                nrm(i, left).wait_recv()
-                pl.when(r > ZL + ZL // 2)(lambda: nrm(i, left).start())
-
-        loop(0, ZL // 2, step)
-        cot_relay(2, start)
-        cot_relay(4, start)
-        loop(ZL // 2, ZL, step)
-        cot_relay(6, start)
-        dispatch(0, nb, send_n, rows_a)
-
-    for d in (1, 3, 5, 7, 8):
-        cot_relay(d, start)
-    dispatch(1, cotb, send_c, rows_c)
+        first = jnp.where(near, 1, 0)
+
+        def take(copy, i):
+            s = jnp.where(near, ZL - 1 - i, i)
+            copy(s, right).wait_recv()
+            pl.when(onward_r)(lambda: copy(s, right).start())
+            pl.when(onward_l)(lambda: copy(s, left).start())
+            return s
+
+        loop(0, ZL // 2, lambda i: to_slots(nb, send_n, take(nrm, i)))
+        go(0, first, send_n, rows_a)
+        loop(ZL // 2, ZL, lambda i: to_slots(nb, send_n, take(nrm, i)))
+        go(0, 1 - first, send_n, rows_a)
+        for n, i in enumerate(chain_order):
+            to_slots(cotb, send_c, take(pass_on, i))
+            if n == enough:
+                go(1, first, send_c, rows_c)
+        go(1, 1 - first, send_c, rows_c)
+
+    keep(send_n, rows_a)
+    keep(send_c, rows_c)
 
     half = pl.ds(pl.multiple_of(c * SL, SL), SL)
     away = pl.ds(pl.multiple_of((1 - c) * SL, SL), SL)
@@ -317,7 +347,8 @@
     here_rows = pl.ds(pl.multiple_of(p * CAP, CAP), CAP)
 
     a_copy = sib(rows_a.at[half], rows_a.at[half], 1)
-    loop(1, NP, lambda k: xy_arrival(0, rows_a, c * SL, k).wait_recv())
+    for h in (0, 1):
+        loop(1, NP, lambda k: xy_arrival(0, h, rows_a, k).wait_recv())
     a_copy.start()
     weight_in = w_in[...]
     weight_out = w_out[...]
@@ -352,8 +383,8 @@
         return remote(
             src.at[pl.ds(pl.multiple_of(c * SL + plane(k, 1) * CAP, CAP), CAP), cols],
             dst.at[here_rows, cols],
-            xy_s.at[2 + 2 * a + h, k],
-            xy_q.at[2 + 2 * a + h, k],
+            xy_s.at[4 + 2 * a + h, k],
+            xy_q.at[4 + 2 * a + h, k],
             plane_id(k),
         )
 
@@ -362,7 +393,7 @@
         cut = wide - D // 2
         cols = pl.ds(0, cut) if h == 0 else pl.ds(cut, D // 2)
         here = dst.at[pl.ds(pl.multiple_of(plane(k, -1) * CAP, CAP), CAP), cols]
-        return remote(here, here, xy_s.at[2 + 2 * a + h, k], xy_q.at[2 + 2 * a + h, k], plane_id(k))
+        return remote(here, here, xy_s.at[4 + 2 * a + h, k], xy_q.at[4 + 2 * a + h, k], plane_id(k))
 
     p_copy = sib(prodb.at[away], sib_p, 3)
     sib(rows_a.at[away], rows_a.at[away], 1).wait_recv()
@@ -376,7 +407,8 @@
     got_p[here_rows, :] = prodb[mine_rows, :]
 
     c_copy = sib(rows_c.at[half], rows_c.at[half], 2)
-    loop(1, NP, lambda k: xy_arrival(1, rows_c, c * SL, k).wait_recv())
+    for h in (0, 1):
+        loop(1, NP, lambda k: xy_arrival(1, h, rows_c, k).wait_recv())
     c_copy.start()
     gain_hi = gain[...].astype(BF16)
     gain_lo = (gain[...] - gain_hi.astype(F32)).astype(BF16)
@@ -490,13 +522,6 @@
         gin[at, :] = jnp.transpose(dot(d_t[...], rows_a[:, at])).astype(BF16)
 
     loop(0, D // W // 2, grads)
-    relays(0, (6, 2), 0, ZL)
-    loop(D // W // 2, D // W, grads)
-    relays(0, (4,), 0, ZL)
-
-    loop(1, NZ, lambda k: v_arrival(k).wait_recv())
-    vp[p, 0, :, :] = jnp.sum(vz[0:ZL], axis=0)
-    vp[p, 1, :, :] = jnp.sum(vz[ZL:NZ], axis=0)
 
     def vp_send(k):
         return remote(vp.at[p], vp.at[p], vz_s.at[1, k], vz_q.at[1, k], plane_id(k))
@@ -505,7 +530,20 @@
         here = vp.at[plane(k, -1)]
         return remote(here, here, vz_s.at[1, k], vz_q.at[1, k], plane_id(k))
 
-    loop(1, NP, lambda k: vp_send(k).start())
+    router_all = routerT[...]
+
+    @pl.when(own)
+    def _():
+        router_h = router_all.astype(BF16)
+        router_l = (router_all - router_h.astype(F32)).astype(BF16)
+        logits = jnp.zeros((E, T), F32)
+        for b in range(ZL):
+            at = slice(b * W, (b + 1) * W)
+            logits += dot(router_h[:, at], nb[b], NT) + dot(router_l[:, at], nb[b], NT)
+        logits_t[...] = logits
+
+    relays(0, (6, 2), 0, ZL)
+    loop(D // W // 2, D // W, grads)
 
     combine(1, 0, got_r)
     extra = jnp.transpose(got_r[:, 0:W].astype(F32)).astype(BF16)
@@ -514,7 +552,6 @@
     scal[z, 0:1, :] = t0[0:1, :]
     scal[z, 1:2, :] = t1[0:1, :]
     scal[z, 2:4, :] = t0[1:3, :] + t1[1:3, :]
-    scal[z, 4:8, :] = jnp.zeros((4, T), F32)
 
     def sc_copy(s):
         to = lax.rem(s + ZL * c, NZ)
@@ -525,10 +562,17 @@
         return remote(here, here, sc_s.at[0], sc_q.at[k], right)
 
     loop(0, ZL, lambda s: pl.when(s != r)(lambda: sc_copy(s).start()))
+    relays(0, (4,), 0, ZL)
     relays(1, (6, 2), 0, ZL // 2)
     combine(1, 1, got_r)
     relays(1, (4,), 0, ZL // 2)
-    relays(1, (6, 2, 4), ZL // 2, ZL)
+    relays(1, (6, 2), ZL // 2, ZL)
+
+    loop(1, NZ, lambda k: v_arrival(k).wait_recv())
+    vp[p, 0, :, :] = jnp.sum(vz[0:ZL], axis=0)
+    vp[p, 1, :, :] = jnp.sum(vz[ZL:NZ], axis=0)
+    loop(1, NP, lambda k: vp_send(k).start())
+    relays(1, (4,), ZL // 2, ZL)
 
     loop(1, NP, lambda k: vp_arrival(k).wait_recv())
     vp_copy = sib(vp, vout.at[c], 6)
@@ -541,13 +585,7 @@
     def _():
         s = lax.rem(r, ZL)
         cols = pl.ds(pl.multiple_of(zl * W, W), W)
-        router_all = routerT[...]
-        router_h = router_all.astype(BF16)
-        router_l = (router_all - router_h.astype(F32)).astype(BF16)
-        logits = jnp.zeros((E, T), F32)
-        for b in range(ZL):
-            at = slice(b * W, (b + 1) * W)
-            logits += dot(router_h[:, at], nb[b], NT) + dot(router_l[:, at], nb[b], NT)
+        logits = logits_t[...]
         r0 = rt[0:1, :].astype(F32)
         r1 = rt[1:2, :].astype(F32)
         ids = lax.broadcasted_iota(jnp.int32, (E, T), 0).astype(F32)
@@ -607,20 +645,20 @@
         pl.when(r == ZL - 1)(lambda: loop(0, ZL, lambda s: nrm(s, right).wait_send()))
         pl.when(r == 0)(lambda: loop(0, ZL, lambda s: nrm(s, left).wait_send()))
         cot_source(sent)
+        for d in order:
+            cot_relay(d, sent, wait=False)
 
     @pl.when(jnp.logical_not(own))
     def _():
         cot_copy.wait_send()
-        pl.when(r < ZL + ZL // 2 - 1)(lambda: loop(0, ZL, lambda s: nrm(s, right).wait_send()))
-        pl.when(r > ZL + ZL // 2)(lambda: loop(0, ZL, lambda s: nrm(s, left).wait_send()))
-
-    for d in (2, 4, 6):
-        cot_relay(d, sent, wait=False)
+        pl.when(onward_r | onward_l)(
+            lambda: loop(0, ZL, lambda s: (nrm(s, right).wait_send(), pass_on(s, right).wait_send()))
+        )
 
     def last_xy(k):
-        xy(0, send_n, rows_a, c * SL, k).wait_send()
-        xy(1, send_c, rows_c, c * SL, k).wait_send()
         for h in (0, 1):
+            xy(0, h, send_n, rows_a, k).wait_send()
+            xy(1, h, send_c, rows_c, k).wait_send()
             give(0, h, prodb, got_p, k).wait_send()
             give(1, h, retb, got_r, k).wait_send()
         vp_send(k).wait_send()
@@ -683,7 +721,8 @@
             pltpu.VMEM((2, ZL, T, W), BF16),
             pltpu.VMEM((2, ZL, 2, T, W), BF16),
             pltpu.VMEM((2, 6, T, W), BF16),
-            pltpu.VMEM((NZ, 8, T), F32),
+            pltpu.VMEM((NZ, 4, T), F32),
+            pltpu.VMEM((E, T), F32),
             pltpu.VMEM((2, D // W, W), F32),
             pltpu.VMEM((D // W, W), F32),
             pltpu.VMEM((NZ, D // W, W), F32),
@@ -694,11 +733,12 @@
             dma((2,)),
             dma((ZL,)),
             dma((ZL,)),
+            dma((ZL,)),
             dma((6,)),
             dma((ZL, 2)),
             dma((ZL,)),
-            dma((6, NP)),
-            dma((6, NP)),
+            dma((8, NP)),
+            dma((8, NP)),
             dma((2, ZL)),
             dma((2, ZL, 2)),
             dma((2, 6)),

time: 149 us -> 137 us (0.919)
  Pallas kernels: 137 us -> 125 us
    pallas_call x1, Pallas kernels: 137 us -> 125 us  [shards(): pl.pallas_call(functools.partial(kernel, dims), out_shape=[jax.ShapeDtype...]
where the time goes in v3:
time: 137 us; the launch traced here: 136 us
  Pallas kernels  125 us (91%)
  local copies, waits for them, and re-layouts  8.72 us (6%)
  other arithmetic  1.6 us (1%)
    pallas_call x1, Pallas kernels, shards(): pl.pallas_call(functools.partial(kernel, dims), out_shape=[jax.ShapeDtype...  125 us
    unnamed x19, local copies, waits for them, and re-layouts  7.51 us

profile of v3, /device:TPU:1, one launch (start us, length us, event | category | flops | bytes accessed | tf_op | source)
XLA Modules:
  0.0 135.9 jit_solution(14087063108296794883)
XLA Ops:
  0.6 0.0 copy-start.6
  0.6 0.7 copy-done.6
  1.3 0.6 pad.4.routesT
  1.9 1.5 %copy.16.cot = bf16[384,64]{1,0:T(8,128)(2,1)} copy(bf16[384,64]{0,1:T(8,128)(2,1)} %param.13) | data formatting | bytes 98304 | tf_op args[6]
  3.5 124.9 %experts.1 = (bf16[384,64]{1,0:T(8,128)(2,1)}, bf16[384,64]{1,0:T(8,128)(2,1)}, f32[2,16,2,8,128]{4,3,2,1,0:T(8,128)}, bf16[1024,256]{1,0:T(8,128)(2,1)}, bf16[256,1024]{1,0:T(8,128)(2,1)}) custom-call(bf16[384,1024]{1,0:T(8,128)(2,1)} %frames.1, f32[1,1024]{1,0:T(1,128)} %bitcast.29, f32[32,1024]{1,0:T(8,128)} %bitcast.23, s32[8,384]{1,0:T(8,128)} %pad.4.routesT, ...), custom_call_target="tpu_custom_call" | custom-call | tf_op jit(solution)/shard_map/experts/pallas_call | solution.py:687
  128.3 0.0 copy-start.3
  128.3 1.6 %copy.18 = bf16[384,64]{0,1:T(8,128)(2,1)} copy(bf16[384,64]{1,0:T(8,128)(2,1)} %get-tuple-element.22) | data formatting | bytes 98304
  130.0 0.9 add_reduce_fusion
  130.9 0.0 copy-done.3
  130.9 0.0 copy-start.4
  130.9 0.0 copy-start
  130.9 0.0 copy-start.2
  131.0 0.9 copy-done
  131.9 0.0 copy-start.5
  131.9 0.7 multiply_reduce_fusion
  132.5 0.0 copy-done.5
  132.6 0.6 dynamic_slice.3
  133.1 0.0 copy-done.4
  133.1 0.7 copy.19
  133.9 0.0 copy-done.2
  133.9 0.0 copy-start.1
  133.9 0.8 copy.25
  134.7 0.4 copy-done.1
  135.1 0.8 copy.26
  (3 shorter events, 0.0 us)
Async XLA Ops:
  0.6 0.7 copy-start.6
  128.3 2.5 %copy-start.3 = (f32[2,16,2,8,128]{4,3,2,1,0:T(8,128)S(1)}, f32[2,16,2,8,128]{4,3,2,1,0:T(8,128)}, u32[]{:S(2)}) copy-start(f32[2,16,2,8,128]{4,3,2,1,0:T(8,128)} %get-tuple-element.13) | copy-start | bytes 786436
  130.9 2.3 %copy-start.4 = (bf16[384,64]{1,0:T(8,128)(2,1)S(1)}, bf16[384,64]{1,0:T(8,128)(2,1)}, u32[]{:S(2)}) copy-start(bf16[384,64]{1,0:T(8,128)(2,1)} %get-tuple-element.23) | copy-start | bytes 147460
  130.9 0.9 copy-start
  130.9 2.9 %copy-start.2 = (bf16[1024,256]{1,0:T(8,128)(2,1)S(1)}, bf16[1024,256]{1,0:T(8,128)(2,1)}, u32[]{:S(2)}) copy-start(bf16[1024,256]{1,0:T(8,128)(2,1)} %get-tuple-element.14) | copy-start | bytes 1572868
  131.9 0.7 copy-start.5
  133.9 1.2 copy-start.1

commit v4 on v3

--- a/solution.py
+++ b/solution.py
@@ -29,6 +29,13 @@
 
 PARENT = {1: 0, 2: 0, 3: 2, 4: 0, 5: 4, 6: 4, 7: 6, 8: 6}
 LAST = {1: 0, 2: 1, 4: 2}
+FLAT = {1: 0, 2: 0, 3: 2, 4: 2, 5: 0, 6: 5, 7: 5, 8: 5}
+TREES = (PARENT, FLAT)
+PARTS = (2, 4)
+
+
+def children(tree, d, most):
+    return [k for k in range(1, most + 1) if tree[k] == d]
 
 
 def kernel(
@@ -42,7 +49,8 @@
     cot,
     mixed,
     dfr,
-    vout,
+    dgain,
+    drouter,
     gin,
     gout,
     rt,
@@ -76,6 +84,7 @@
     sibvw,
     vz,
     vp,
+    vout,
     tail,
     sib_s,
     sib_q,
@@ -291,15 +300,15 @@
         pl.when(r == ZL - 1)(lambda: loop(0, ZL, lambda i: nrm(ZL - 1 - i, right).start()))
         pl.when(r == 0)(lambda: loop(0, ZL, lambda s: nrm(s, left).start()))
         cot_copy.wait_recv()
-        one, two = cot[...], sibcot[...]
+        one, two = cot[...].astype(F32), sibcot[...].astype(F32)
 
         @pl.when(c == 0)
         def _():
-            cotb[r, :, :] = jnp.concatenate([one, two], axis=1)
+            cotb[r, :, :] = jnp.transpose(jnp.concatenate([one, two], axis=0)).astype(BF16)
 
         @pl.when(c == 1)
         def _():
-            cotb[r, :, :] = jnp.concatenate([two, one], axis=1)
+            cotb[r, :, :] = jnp.transpose(jnp.concatenate([two, one], axis=0)).astype(BF16)
 
         cot_source(start)
         positions()
@@ -376,10 +385,13 @@
         mine = pl.ds(pl.multiple_of(c * SL + i * RT, RT), RT)
         buf[mine, :] = (buf[mine, :].astype(F32) + other[at, :].astype(F32)).astype(BF16)
 
+    def part_cols(a, h):
+        off = a * W
+        step = D // PARTS[a]
+        return pl.ds(off + h * step, step) if h else pl.ds(0, off + step)
+
     def give(a, h, src, dst, k):
-        wide = src.shape[1]
-        cut = wide - D // 2
-        cols = pl.ds(0, cut) if h == 0 else pl.ds(cut, D // 2)
+        cols = part_cols(a, h)
         return remote(
             src.at[pl.ds(pl.multiple_of(c * SL + plane(k, 1) * CAP, CAP), CAP), cols],
             dst.at[here_rows, cols],
@@ -389,10 +401,7 @@
         )
 
     def give_arrival(a, h, dst, k):
-        wide = dst.shape[1]
-        cut = wide - D // 2
-        cols = pl.ds(0, cut) if h == 0 else pl.ds(cut, D // 2)
-        here = dst.at[pl.ds(pl.multiple_of(plane(k, -1) * CAP, CAP), CAP), cols]
+        here = dst.at[pl.ds(pl.multiple_of(plane(k, -1) * CAP, CAP), CAP), part_cols(a, h)]
         return remote(here, here, xy_s.at[4 + 2 * a + h, k], xy_q.at[4 + 2 * a + h, k], plane_id(k))
 
     p_copy = sib(prodb.at[away], sib_p, 3)
@@ -451,7 +460,7 @@
     v_copy.start()
     r_copy.wait_recv()
     loop(0, tiles, lambda i: pair_sum(retb, sib_r, i))
-    for h in (0, 1):
+    for h in range(PARTS[1]):
         loop(1, NP, lambda k: give(1, h, retb, got_r, k).start())
     got_r[here_rows, :] = retb[mine_rows, :]
 
@@ -468,6 +477,7 @@
     loop(1, NZ, lambda k: v_send(k).start())
 
     def up(a, d, lo, hi, act, run=True):
+        tree = TREES[a]
         for way in (0, 1):
             if d > reach[way]:
                 continue
@@ -476,42 +486,44 @@
             @pl.when((to >= lo) & (to < hi))
             def _():
                 s = lax.rem(to, ZL)
-                pd = PARENT[d]
+                pd = tree[d]
+                q = children(tree, pd, reach[way]).index(d)
                 if pd == 0:
-                    dst, sem = fin.at[a, way * 3 + LAST[d]], fin_q.at[a, way * 3 + LAST[d]]
+                    dst, sem = fin.at[a, way * 3 + q], fin_q.at[a, way * 3 + q]
                 else:
-                    dst, sem = relay.at[a, s, 1 - d % 2], relay_q.at[a, s, 1 - d % 2]
+                    dst, sem = relay.at[a, s, q], relay_q.at[a, s, q]
                 if run:
-                    kids = [k for k in (d + 1, d + 2) if k <= reach[way] and PARENT[k] == d]
+                    kids = children(tree, d, reach[way])
                     total = None
-                    for kid in kids:
-                        q = 1 - kid % 2
-                        landed = relay.at[a, s, q]
-                        remote(landed, landed, up_s.at[a, s], relay_q.at[a, s, q], right).wait_recv()
+                    for n in range(len(kids)):
+                        landed = relay.at[a, s, n]
+                        remote(landed, landed, up_s.at[a, s], relay_q.at[a, s, n], right).wait_recv()
                         if total is None:
                             total = part[a, s, :, :].astype(F32)
-                        total = total + relay[a, s, q, :, :].astype(F32)
+                        total = total + relay[a, s, n, :, :].astype(F32)
                     if kids:
                         part[a, s, :, :] = total.astype(BF16)
                 act(remote(part.at[a, s], dst, up_s.at[a, s], sem, z_at(way, d - pd)))
 
     def combine(a, h, got):
-        first = h * (ZL // 2)
-        off = got.shape[1] - D
+        count = ZL // PARTS[a]
+        first = h * count
 
         def one(i):
             s = first + i
-            at = pl.ds(pl.multiple_of(off + s * W, W), W)
+            at = pl.ds(pl.multiple_of(a * W + s * W, W), W)
             part[a, s, :, :] = dot(pcomb[...], got[:, at]).astype(BF16)
 
         loop(1, NP, lambda k: give_arrival(a, h, got, k).wait_recv())
-        loop(0, ZL // 2, one)
-        for d in (7, 8, 5, 3, 1):
-            up(a, d, first, first + ZL // 2, start)
+        loop(0, count, one)
+        for d in (8, 7, 6, 5, 4, 3, 1, 2):
+            if d <= ZL and not children(TREES[a], d, 8):
+                up(a, d, first, first + count, start)
 
     def relays(a, ds, lo, hi):
         for d in ds:
-            up(a, d, lo, hi, start)
+            if d <= ZL:
+                up(a, d, lo, hi, start)
 
     combine(0, 0, got_p)
     combine(0, 1, got_p)
@@ -563,28 +575,56 @@
 
     loop(0, ZL, lambda s: pl.when(s != r)(lambda: sc_copy(s).start()))
     relays(0, (4,), 0, ZL)
-    relays(1, (6, 2), 0, ZL // 2)
-    combine(1, 1, got_r)
-    relays(1, (4,), 0, ZL // 2)
-    relays(1, (6, 2), ZL // 2, ZL)
-
     loop(1, NZ, lambda k: v_arrival(k).wait_recv())
     vp[p, 0, :, :] = jnp.sum(vz[0:ZL], axis=0)
     vp[p, 1, :, :] = jnp.sum(vz[ZL:NZ], axis=0)
     loop(1, NP, lambda k: vp_send(k).start())
-    relays(1, (4,), ZL // 2, ZL)
+    quarter = ZL // PARTS[1]
+
+    def relays_q(h):
+        relays(1, (5, 2), h * quarter, (h + 1) * quarter)
+
+    combine(1, 1, got_r)
+    relays_q(0)
+    combine(1, 2, got_r)
+    relays_q(1)
 
     loop(1, NP, lambda k: vp_arrival(k).wait_recv())
     vp_copy = sib(vp, vout.at[c], 6)
     vp_copy.start()
     vout[c, :, :, :, :] = vp[...]
 
+    combine(1, 3, got_r)
+    relays_q(2)
+
+    cols = pl.ds(pl.multiple_of(zl * W, W), W)
+    sib(vp, vout.at[1 - c], 6).wait_recv()
+    for q in range(NP):
+        for up_half in (0, 1):
+            e = up_half * NP + q
+            for b in range(D // W):
+                drouter[e : e + 1, b * W : (b + 1) * W] = vout[0, q, up_half, b : b + 1, :] * (1.0 / T)
+    sibvw[...] = jnp.sum(jnp.sum(vout[1], axis=0), axis=0) * (1.0 / T)
+    d_gain = sibvw[pl.ds(zl, 1), :] + jnp.sum(
+        routerT[:, cols] * drouter[:, cols], axis=0, keepdims=True
+    )
+    d_gain = d_gain / gain[:, cols]
+
+    @pl.when(c == 0)
+    def _():
+        dgain[...] = d_gain[:, 0 : W // 2]
+
+    @pl.when(c == 1)
+    def _():
+        dgain[...] = d_gain[:, W // 2 : W]
+
+    relays_q(3)
+
     t_copy = sib(tail, tail, 7)
 
     @pl.when(own)
     def _():
         s = lax.rem(r, ZL)
-        cols = pl.ds(pl.multiple_of(zl * W, W), W)
         logits = logits_t[...]
         r0 = rt[0:1, :].astype(F32)
         r1 = rt[1:2, :].astype(F32)
@@ -612,31 +652,39 @@
         def arrived_sum(a):
             total = part[a, s, :, :].astype(F32)
             for way in (0, 1):
-                for d in (1, 2, 4):
-                    if d <= reach[way]:
-                        q = way * 3 + LAST[d]
-                        landed = fin.at[a, q]
-                        remote(landed, landed, up_s.at[a, s], fin_q.at[a, q], right).wait_recv()
-                        total = total + fin[a, q, :, :].astype(F32)
+                for q in range(len(children(TREES[a], 0, reach[way]))):
+                    landed = fin.at[a, way * 3 + q]
+                    sem = fin_q.at[a, way * 3 + q]
+                    remote(landed, landed, up_s.at[a, s], sem, right).wait_recv()
+                    total = total + fin[a, way * 3 + q, :, :].astype(F32)
             return total
 
-        tail[0, :, :] = (values + arrived_sum(0)).astype(BF16)
+        out_m = jnp.transpose(values + arrived_sum(0)).astype(BF16)
         d_scaled = (arrived_sum(1) + second) * gain[:, cols]
         result = cotb[s, :, :].astype(F32) + inverse * (d_scaled - sum_1 - scaled * sum_2)
-        tail[1, :, :] = result.astype(BF16)
+        out_d = jnp.transpose(result).astype(BF16)
+
+        @pl.when(c == 0)
+        def _():
+            tail[0, :, :] = out_m[W // 2 : W, :]
+            tail[1, :, :] = out_d[W // 2 : W, :]
+            mixed[...] = out_m[0 : W // 2, :]
+            dfr[...] = out_d[0 : W // 2, :]
+
+        @pl.when(c == 1)
+        def _():
+            tail[0, :, :] = out_m[0 : W // 2, :]
+            tail[1, :, :] = out_d[0 : W // 2, :]
+            mixed[...] = out_m[W // 2 : W, :]
+            dfr[...] = out_d[W // 2 : W, :]
+
         t_copy.start()
 
-    pl.when(jnp.logical_not(own))(lambda: t_copy.wait_recv())
-
-    @pl.when(c == 0)
-    def _():
-        mixed[...] = tail[0, :, 0 : W // 2]
-        dfr[...] = tail[1, :, 0 : W // 2]
-
-    @pl.when(c == 1)
-    def _():
-        mixed[...] = tail[0, :, W // 2 : W]
-        dfr[...] = tail[1, :, W // 2 : W]
+    @pl.when(jnp.logical_not(own))
+    def _():
+        t_copy.wait_recv()
+        mixed[...] = tail[0, :, :]
+        dfr[...] = tail[1, :, :]
 
     @pl.when(own)
     def _():
@@ -660,6 +708,7 @@
             xy(0, h, send_n, rows_a, k).wait_send()
             xy(1, h, send_c, rows_c, k).wait_send()
             give(0, h, prodb, got_p, k).wait_send()
+        for h in range(PARTS[1]):
             give(1, h, retb, got_r, k).wait_send()
         vp_send(k).wait_send()
 
@@ -669,7 +718,6 @@
     for d in range(1, ZL + 1):
         for a in (0, 1):
             up(a, d, 0, ZL, sent, run=False)
-    sib(vp, vout.at[1 - c], 6).wait_recv()
     for copy in (a_copy, c_copy, p_copy, r_copy, v_copy, vp_copy):
         copy.wait_send()
 
@@ -684,22 +732,23 @@
     HS = w_in.shape[2]
     vmem = pl.BlockSpec(memory_space=pltpu.VMEM)
     dma = pltpu.SemaphoreType.DMA
-    mixed, dfr, sums, gin, gout = pl.pallas_call(
+    mixed, dfr, d_gain, d_router, gin, gout = pl.pallas_call(
         functools.partial(kernel, dims),
         out_shape=[
-            jax.ShapeDtypeStruct((T, W // 2), BF16),
-            jax.ShapeDtypeStruct((T, W // 2), BF16),
-            jax.ShapeDtypeStruct((2, NP, 2, D // W, W), F32),
+            jax.ShapeDtypeStruct((W // 2, T), BF16),
+            jax.ShapeDtypeStruct((W // 2, T), BF16),
+            jax.ShapeDtypeStruct((1, W // 2), F32),
+            jax.ShapeDtypeStruct((E, D), F32),
             jax.ShapeDtypeStruct((D, HS), BF16),
             jax.ShapeDtypeStruct((HS, D), BF16),
         ],
         in_specs=[vmem] * 7,
-        out_specs=[vmem] * 5,
+        out_specs=[vmem] * 6,
         scratch_shapes=[
             pltpu.VMEM((8, T), jnp.int32),
             pltpu.VMEM((ZL, T, W), BF16),
             pltpu.VMEM((ZL, T, W), BF16),
-            pltpu.VMEM((T, W // 2), BF16),
+            pltpu.VMEM((W // 2, T), BF16),
             pltpu.VMEM((2, T, W), F32),
             pltpu.VMEM((SL, T), BF16),
             pltpu.VMEM((SL, T), BF16),
@@ -719,7 +768,7 @@
             pltpu.VMEM((SL, D), BF16),
             pltpu.VMEM((SL, D + W), BF16),
             pltpu.VMEM((2, ZL, T, W), BF16),
-            pltpu.VMEM((2, ZL, 2, T, W), BF16),
+            pltpu.VMEM((2, ZL, 3, T, W), BF16),
             pltpu.VMEM((2, 6, T, W), BF16),
             pltpu.VMEM((NZ, 4, T), F32),
             pltpu.VMEM((E, T), F32),
@@ -727,7 +776,8 @@
             pltpu.VMEM((D // W, W), F32),
             pltpu.VMEM((NZ, D // W, W), F32),
             pltpu.VMEM((NP, 2, D // W, W), F32),
-            pltpu.VMEM((2, T, W), BF16),
+            pltpu.VMEM((2, NP, 2, D // W, W), F32),
+            pltpu.VMEM((2, W // 2, T), BF16),
             dma((8,)),
             dma((8,)),
             dma((2,)),
@@ -737,10 +787,10 @@
             dma((6,)),
             dma((ZL, 2)),
             dma((ZL,)),
-            dma((8, NP)),
-            dma((8, NP)),
+            dma((10, NP)),
+            dma((10, NP)),
             dma((2, ZL)),
-            dma((2, ZL, 2)),
+            dma((2, ZL, 3)),
             dma((2, 6)),
             dma((ZL,)),
             dma((NZ,)),
@@ -758,15 +808,10 @@
         jnp.pad(routes.T, ((0, 8 - routes.shape[1]), (0, 0))),
         w_in.reshape(D, HS),
         w_out.reshape(HS, D),
-        cotangent,
+        cotangent.T,
     )
-    column = lax.axis_index("expert")
-    router_sum = sums[0].transpose(1, 0, 2, 3).reshape(E, D)
-    d_router = router_sum.T * (1.0 / T)
-    gain_sum = jnp.sum(sums[1, :, 0] + sums[1, :, 1], axis=0).reshape(D) * (1.0 / T)
-    d_gain = (gain_sum + jnp.sum(router * d_router, axis=1)) / norm_gain
-    d_gain = lax.dynamic_slice_in_dim(d_gain, column * (W // 2), W // 2, 0)
-    return mixed, dfr, d_gain, d_router, gin.reshape(1, D, HS), gout.reshape(1, HS, D)
+    d_gain = d_gain.reshape(W // 2)
+    return mixed.T, dfr.T, d_gain, d_router.T, gin.reshape(1, D, HS), gout.reshape(1, HS, D)
 
 
 def plan(mesh):

time: 137 us -> 133 us (0.971)
  the two profiles are of different devices: /device:TPU:1 before, /device:TPU:111 now
where the time goes in v4:
time: 133 us
  Pallas kernels  124 us (93%)
  local copies, waits for them, and re-layouts  8.06 us (6%)
    pallas_call x1, Pallas kernels, shards(): pl.pallas_call(functools.partial(kernel, dims), out_shape=[jax.ShapeDtype...  124 us
    unnamed x14, local copies, waits for them, and re-layouts  7.46 us

profile of v4, /device:TPU:111, one launch (start us, length us, event | category | flops | bytes accessed | tf_op | source)
XLA Modules:
  0.0 132.5 jit_solution(18368233957523983407)
XLA Ops:
  0.6 0.0 copy-start.2
  0.6 0.7 copy-done.2
  1.3 0.6 pad.4.routesT
  1.9 123.8 %experts.1 = (bf16[64,384]{1,0:T(8,128)(2,1)}, bf16[64,384]{1,0:T(8,128)(2,1)}, f32[1,64]{1,0:T(1,128)}, f32[32,1024]{1,0:T(8,128)}, bf16[1024,256]{1,0:T(8,128)(2,1)}, /*index=5*/bf16[256,1024]{1,0:T(8,128)(2,1)}) custom-call(bf16[384,1024]{1,0:T(8,128)(2,1)} %frames.1, f32[1,1024]{1,0:T(1,128)} %bitcast.21, f32[32,1024]{1,0:T(8,128)} %bitcast.16, ...), custom_call_target="tpu_custom_call" | custom-call | tf_op jit(solution)/shard_map/experts/pallas_call | solution.py:735
  125.7 0.0 copy-start.1
  125.7 1.5 %copy.19 = bf16[384,64]{0,1:T(8,128)(2,1)} copy(bf16[384,64]{0,1:T(8,128)(2,1)} %bitcast.19) | data formatting | bytes 98304
  127.2 0.0 copy-start.3
  127.2 1.4 %copy.20 = bf16[384,64]{0,1:T(8,128)(2,1)} copy(bf16[384,64]{0,1:T(8,128)(2,1)} %bitcast.18) | data formatting | bytes 98304
  128.6 0.0 copy-done.3
  128.6 0.5 copy.21
  129.1 0.0 copy-done.1
  129.1 0.7 copy.22
  129.8 0.0 copy-start
  129.8 1.9 %copy.23 = bf16[1,1024,256]{2,1,0:T(8,128)(2,1)} copy(bf16[1,1024,256]{2,1,0:T(8,128)(2,1)} %bitcast.13) | data formatting | bytes 1048576
  131.7 0.0 copy-done
  131.7 0.8 copy.24
Async XLA Ops:
  0.6 0.7 copy-start.2
  125.7 3.4 %copy-start.1 = (f32[32,1024]{1,0:T(8,128)S(1)}, f32[32,1024]{1,0:T(8,128)}, u32[]{:S(2)}) copy-start(f32[32,1024]{1,0:T(8,128)} %get-tuple-element.15) | copy-start | bytes 393220
  127.2 1.4 %copy-start.3 = (f32[1,64]{1,0:T(1,128)S(1)}, f32[1,64]{1,0:T(1,128)}, u32[]{:S(2)}) copy-start(f32[1,64]{1,0:T(1,128)} %get-tuple-element.14) | copy-start | bytes 772
  129.8 1.9 %copy-start = (bf16[256,1024]{1,0:T(8,128)(2,1)S(1)}, bf16[256,1024]{1,0:T(8,128)(2,1)}, u32[]{:S(2)}) copy-start(bf16[256,1024]{1,0:T(8,128)(2,1)} %get-tuple-element.17) | copy-start | bytes 1572868

commit v5 on v4

--- a/solution.py
+++ b/solution.py
@@ -29,13 +29,15 @@
 
 PARENT = {1: 0, 2: 0, 3: 2, 4: 0, 5: 4, 6: 4, 7: 6, 8: 6}
 LAST = {1: 0, 2: 1, 4: 2}
-FLAT = {1: 0, 2: 0, 3: 2, 4: 2, 5: 0, 6: 5, 7: 5, 8: 5}
-TREES = (PARENT, FLAT)
-PARTS = (2, 4)
+SUM_TREE = {1: 0, 2: 1, 3: 2, 4: 0, 5: 4, 6: 5, 7: 4, 8: 7}
 
 
 def children(tree, d, most):
     return [k for k in range(1, most + 1) if tree[k] == d]
+
+
+def height(tree, d, most):
+    return max([1 + height(tree, k, most) for k in children(tree, d, most)], default=0)
 
 
 def kernel(
@@ -385,24 +387,18 @@
         mine = pl.ds(pl.multiple_of(c * SL + i * RT, RT), RT)
         buf[mine, :] = (buf[mine, :].astype(F32) + other[at, :].astype(F32)).astype(BF16)
 
-    def part_cols(a, h):
-        off = a * W
-        step = D // PARTS[a]
-        return pl.ds(off + h * step, step) if h else pl.ds(0, off + step)
-
-    def give(a, h, src, dst, k):
-        cols = part_cols(a, h)
+    def give(a, src, dst, k):
         return remote(
-            src.at[pl.ds(pl.multiple_of(c * SL + plane(k, 1) * CAP, CAP), CAP), cols],
-            dst.at[here_rows, cols],
-            xy_s.at[4 + 2 * a + h, k],
-            xy_q.at[4 + 2 * a + h, k],
+            src.at[pl.ds(pl.multiple_of(c * SL + plane(k, 1) * CAP, CAP), CAP)],
+            dst.at[here_rows],
+            xy_s.at[4 + a, k],
+            xy_q.at[4 + a, k],
             plane_id(k),
         )
 
-    def give_arrival(a, h, dst, k):
-        here = dst.at[pl.ds(pl.multiple_of(plane(k, -1) * CAP, CAP), CAP), part_cols(a, h)]
-        return remote(here, here, xy_s.at[4 + 2 * a + h, k], xy_q.at[4 + 2 * a + h, k], plane_id(k))
+    def give_arrival(a, dst, k):
+        here = dst.at[pl.ds(pl.multiple_of(plane(k, -1) * CAP, CAP), CAP)]
+        return remote(here, here, xy_s.at[4 + a, k], xy_q.at[4 + a, k], plane_id(k))
 
     p_copy = sib(prodb.at[away], sib_p, 3)
     sib(rows_a.at[away], rows_a.at[away], 1).wait_recv()
@@ -411,8 +407,7 @@
     loop(0, tiles, lambda i: forward(c * tiles + i))
     p_copy.wait_recv()
     loop(0, tiles, lambda i: pair_sum(prodb, sib_p, i))
-    for h in (0, 1):
-        loop(1, NP, lambda k: give(0, h, prodb, got_p, k).start())
+    loop(1, NP, lambda k: give(0, prodb, got_p, k).start())
     got_p[here_rows, :] = prodb[mine_rows, :]
 
     c_copy = sib(rows_c.at[half], rows_c.at[half], 2)
@@ -460,8 +455,7 @@
     v_copy.start()
     r_copy.wait_recv()
     loop(0, tiles, lambda i: pair_sum(retb, sib_r, i))
-    for h in range(PARTS[1]):
-        loop(1, NP, lambda k: give(1, h, retb, got_r, k).start())
+    loop(1, NP, lambda k: give(1, retb, got_r, k).start())
     got_r[here_rows, :] = retb[mine_rows, :]
 
     v_copy.wait_recv()
@@ -476,57 +470,44 @@
 
     loop(1, NZ, lambda k: v_send(k).start())
 
-    def up(a, d, lo, hi, act, run=True):
-        tree = TREES[a]
-        for way in (0, 1):
-            if d > reach[way]:
-                continue
-            to = lax.rem(r + (d if way == 0 else NZ - d), NZ)
-
-            @pl.when((to >= lo) & (to < hi))
-            def _():
-                s = lax.rem(to, ZL)
-                pd = tree[d]
-                q = children(tree, pd, reach[way]).index(d)
-                if pd == 0:
-                    dst, sem = fin.at[a, way * 3 + q], fin_q.at[a, way * 3 + q]
-                else:
-                    dst, sem = relay.at[a, s, q], relay_q.at[a, s, q]
-                if run:
-                    kids = children(tree, d, reach[way])
-                    total = None
-                    for n in range(len(kids)):
-                        landed = relay.at[a, s, n]
-                        remote(landed, landed, up_s.at[a, s], relay_q.at[a, s, n], right).wait_recv()
-                        if total is None:
-                            total = part[a, s, :, :].astype(F32)
-                        total = total + relay[a, s, n, :, :].astype(F32)
-                    if kids:
-                        part[a, s, :, :] = total.astype(BF16)
-                act(remote(part.at[a, s], dst, up_s.at[a, s], sem, z_at(way, d - pd)))
-
-    def combine(a, h, got):
-        count = ZL // PARTS[a]
-        first = h * count
-
-        def one(i):
-            s = first + i
+    def up(a, d, way, act, run=True):
+        to = lax.rem(r + (d if way == 0 else NZ - d), NZ)
+
+        @pl.when(to < ZL)
+        def _():
+            s = lax.rem(to, ZL)
+            pd = SUM_TREE[d]
+            q = children(SUM_TREE, pd, reach[way]).index(d)
+            if pd == 0:
+                dst, sem = fin.at[a, way * 3 + q], fin_q.at[a, way * 3 + q]
+            else:
+                dst, sem = relay.at[a, s, q], relay_q.at[a, s, q]
+            kids = children(SUM_TREE, d, reach[way])
+            if run and kids:
+                total = part[a, s, :, :].astype(F32)
+                for n in range(len(kids)):
+                    landed = relay.at[a, s, n]
+                    remote(landed, landed, up_s.at[a, s], relay_q.at[a, s, n], right).wait_recv()
+                    total = total + relay[a, s, n, :, :].astype(F32)
+                part[a, s, :, :] = total.astype(BF16)
+            act(remote(part.at[a, s], dst, up_s.at[a, s], sem, z_at(way, d - pd)))
+
+    def stage(a, level):
+        for d in range(ZL, 0, -1):
+            for way in (0, 1):
+                if d <= reach[way] and height(SUM_TREE, d, reach[way]) == level:
+                    up(a, d, way, start)
+
+    def combine(a, got):
+        def one(s):
             at = pl.ds(pl.multiple_of(a * W + s * W, W), W)
             part[a, s, :, :] = dot(pcomb[...], got[:, at]).astype(BF16)
 
-        loop(1, NP, lambda k: give_arrival(a, h, got, k).wait_recv())
-        loop(0, count, one)
-        for d in (8, 7, 6, 5, 4, 3, 1, 2):
-            if d <= ZL and not children(TREES[a], d, 8):
-                up(a, d, first, first + count, start)
-
-    def relays(a, ds, lo, hi):
-        for d in ds:
-            if d <= ZL:
-                up(a, d, lo, hi, start)
-
-    combine(0, 0, got_p)
-    combine(0, 1, got_p)
+        loop(1, NP, lambda k: give_arrival(a, got, k).wait_recv())
+        loop(0, ZL, one)
+        stage(a, 0)
+
+    combine(0, got_p)
 
     def grads(i):
         at = pl.ds(pl.multiple_of(i * W, W), W)
@@ -554,10 +535,15 @@
             logits += dot(router_h[:, at], nb[b], NT) + dot(router_l[:, at], nb[b], NT)
         logits_t[...] = logits
 
-    relays(0, (6, 2), 0, ZL)
+    stage(0, 1)
     loop(D // W // 2, D // W, grads)
-
-    combine(1, 0, got_r)
+    loop(1, NZ, lambda k: v_arrival(k).wait_recv())
+    vp[p, 0, :, :] = jnp.sum(vz[0:ZL], axis=0)
+    vp[p, 1, :, :] = jnp.sum(vz[ZL:NZ], axis=0)
+    loop(1, NP, lambda k: vp_send(k).start())
+    stage(0, 2)
+
+    combine(1, got_r)
     extra = jnp.transpose(got_r[:, 0:W].astype(F32)).astype(BF16)
     t0 = dot(extra, p0t[...])
     t1 = dot(extra, p1t[...])
@@ -574,28 +560,12 @@
         return remote(here, here, sc_s.at[0], sc_q.at[k], right)
 
     loop(0, ZL, lambda s: pl.when(s != r)(lambda: sc_copy(s).start()))
-    relays(0, (4,), 0, ZL)
-    loop(1, NZ, lambda k: v_arrival(k).wait_recv())
-    vp[p, 0, :, :] = jnp.sum(vz[0:ZL], axis=0)
-    vp[p, 1, :, :] = jnp.sum(vz[ZL:NZ], axis=0)
-    loop(1, NP, lambda k: vp_send(k).start())
-    quarter = ZL // PARTS[1]
-
-    def relays_q(h):
-        relays(1, (5, 2), h * quarter, (h + 1) * quarter)
-
-    combine(1, 1, got_r)
-    relays_q(0)
-    combine(1, 2, got_r)
-    relays_q(1)
-
     loop(1, NP, lambda k: vp_arrival(k).wait_recv())
     vp_copy = sib(vp, vout.at[c], 6)
     vp_copy.start()
     vout[c, :, :, :, :] = vp[...]
 
-    combine(1, 3, got_r)
-    relays_q(2)
+    stage(1, 1)
 
     cols = pl.ds(pl.multiple_of(zl * W, W), W)
     sib(vp, vout.at[1 - c], 6).wait_recv()
@@ -618,7 +588,7 @@
     def _():
         dgain[...] = d_gain[:, W // 2 : W]
 
-    relays_q(3)
+    stage(1, 2)
 
     t_copy = sib(tail, tail, 7)
 
@@ -652,7 +622,7 @@
         def arrived_sum(a):
             total = part[a, s, :, :].astype(F32)
             for way in (0, 1):
-                for q in range(len(children(TREES[a], 0, reach[way]))):
+                for q in range(len(children(SUM_TREE, 0, reach[way]))):
                     landed = fin.at[a, way * 3 + q]
                     sem = fin_q.at[a, way * 3 + q]
                     remote(landed, landed, up_s.at[a, s], sem, right).wait_recv()
@@ -707,9 +677,8 @@
         for h in (0, 1):
             xy(0, h, send_n, rows_a, k).wait_send()
             xy(1, h, send_c, rows_c, k).wait_send()
-            give(0, h, prodb, got_p, k).wait_send()
-        for h in range(PARTS[1]):
-            give(1, h, retb, got_r, k).wait_send()
+        give(0, prodb, got_p, k).wait_send()
+        give(1, retb, got_r, k).wait_send()
         vp_send(k).wait_send()
 
     loop(1, NP, last_xy)
@@ -717,7 +686,9 @@
     loop(0, ZL, lambda s: pl.when(s != r)(lambda: sc_copy(s).wait_send()))
     for d in range(1, ZL + 1):
         for a in (0, 1):
-            up(a, d, 0, ZL, sent, run=False)
+            for way in (0, 1):
+                if d <= reach[way]:
+                    up(a, d, way, sent, run=False)
     for copy in (a_copy, c_copy, p_copy, r_copy, v_copy, vp_copy):
         copy.wait_send()
 
@@ -787,8 +758,8 @@
             dma((6,)),
             dma((ZL, 2)),
             dma((ZL,)),
-            dma((10, NP)),
-            dma((10, NP)),
+            dma((6, NP)),
+            dma((6, NP)),
             dma((2, ZL)),
             dma((2, ZL, 3)),
             dma((2, 6)),

time: 133 us -> 142 us (1.068)
  the two profiles are of different devices: /device:TPU:111 before, /device:TPU:1 now
where the time goes in v5:
time: 142 us
  Pallas kernels  133 us (94%)
  local copies, waits for them, and re-layouts  8.06 us (6%)
    pallas_call x1, Pallas kernels, shards(): pl.pallas_call(functools.partial(kernel, dims), out_shape=[jax.ShapeDtype...  133 us
    unnamed x14, local copies, waits for them, and re-layouts  7.46 us

profile of v5, /device:TPU:1, one launch (start us, length us, event | category | flops | bytes accessed | tf_op | source)
XLA Modules:
  0.0 142.2 jit_solution(4070027040974803438)
XLA Ops:
  0.6 0.0 copy-start.2
  0.6 0.7 copy-done.2
  1.3 0.6 pad.4.routesT
  1.9 133.4 %experts.1 = (bf16[64,384]{1,0:T(8,128)(2,1)}, bf16[64,384]{1,0:T(8,128)(2,1)}, f32[1,64]{1,0:T(1,128)}, f32[32,1024]{1,0:T(8,128)}, bf16[1024,256]{1,0:T(8,128)(2,1)}, /*index=5*/bf16[256,1024]{1,0:T(8,128)(2,1)}) custom-call(bf16[384,1024]{1,0:T(8,128)(2,1)} %frames.1, f32[1,1024]{1,0:T(1,128)} %bitcast.21, f32[32,1024]{1,0:T(8,128)} %bitcast.16, ...), custom_call_target="tpu_custom_call" | custom-call | tf_op jit(solution)/shard_map/experts/pallas_call | solution.py:706
  135.4 0.0 copy-start.1
  135.4 1.5 %copy.19 = bf16[384,64]{0,1:T(8,128)(2,1)} copy(bf16[384,64]{0,1:T(8,128)(2,1)} %bitcast.19) | data formatting | bytes 98304
  136.8 0.0 copy-start.3
  136.8 1.4 %copy.20 = bf16[384,64]{0,1:T(8,128)(2,1)} copy(bf16[384,64]{0,1:T(8,128)(2,1)} %bitcast.18) | data formatting | bytes 98304
  138.3 0.0 copy-done.3
  138.3 0.5 copy.21
  138.8 0.0 copy-done.1
  138.8 0.7 copy.22
  139.4 0.0 copy-start
  139.4 1.9 %copy.23 = bf16[1,1024,256]{2,1,0:T(8,128)(2,1)} copy(bf16[1,1024,256]{2,1,0:T(8,128)(2,1)} %bitcast.13) | data formatting | bytes 1048576
  141.4 0.0 copy-done
  141.4 0.8 copy.24
Async XLA Ops:
  0.6 0.7 copy-start.2
  135.4 3.4 %copy-start.1 = (f32[32,1024]{1,0:T(8,128)S(1)}, f32[32,1024]{1,0:T(8,128)}, u32[]{:S(2)}) copy-start(f32[32,1024]{1,0:T(8,128)} %get-tuple-element.15) | copy-start | bytes 393220
  136.8 1.4 %copy-start.3 = (f32[1,64]{1,0:T(1,128)S(1)}, f32[1,64]{1,0:T(1,128)}, u32[]{:S(2)}) copy-start(f32[1,64]{1,0:T(1,128)} %get-tuple-element.14) | copy-start | bytes 772
  139.4 1.9 %copy-start = (bf16[256,1024]{1,0:T(8,128)(2,1)S(1)}, bf16[256,1024]{1,0:T(8,128)(2,1)}, u32[]{:S(2)}) copy-start(bf16[256,1024]{1,0:T(8,128)(2,1)} %get-tuple-element.17) | copy-start | bytes 1572868

commit v6 on v4

--- a/solution.py
+++ b/solution.py
@@ -585,9 +585,8 @@
         relays(1, (5, 2), h * quarter, (h + 1) * quarter)
 
     combine(1, 1, got_r)
+    combine(1, 2, got_r)
     relays_q(0)
-    combine(1, 2, got_r)
-    relays_q(1)
 
     loop(1, NP, lambda k: vp_arrival(k).wait_recv())
     vp_copy = sib(vp, vout.at[c], 6)
@@ -595,7 +594,7 @@
     vout[c, :, :, :, :] = vp[...]
 
     combine(1, 3, got_r)
-    relays_q(2)
+    relays_q(1)
 
     cols = pl.ds(pl.multiple_of(zl * W, W), W)
     sib(vp, vout.at[1 - c], 6).wait_recv()
@@ -618,6 +617,7 @@
     def _():
         dgain[...] = d_gain[:, W // 2 : W]
 
+    relays_q(2)
     relays_q(3)
 
     t_copy = sib(tail, tail, 7)
@@ -745,7 +745,7 @@
         in_specs=[vmem] * 7,
         out_specs=[vmem] * 6,
         scratch_shapes=[
-            pltpu.VMEM((8, T), jnp.int32),
+            pltpu.VMEM((routes.shape[1], T), jnp.int32),
             pltpu.VMEM((ZL, T, W), BF16),
             pltpu.VMEM((ZL, T, W), BF16),
             pltpu.VMEM((W // 2, T), BF16),
@@ -805,7 +805,7 @@
         frames,
         norm_gain.reshape(1, D),
         router.T,
-        jnp.pad(routes.T, ((0, 8 - routes.shape[1]), (0, 0))),
+        routes.T,
         w_in.reshape(D, HS),
         w_out.reshape(HS, D),
         cotangent.T,

time: 133 us -> 132 us (level)
  the two profiles are of different devices: /device:TPU:111 before, /device:TPU:97 now
where the time goes in v6:
time: 132 us; the launch traced here: 131 us
  Pallas kernels  124 us (94%)
  local copies, waits for them, and re-layouts  6.78 us (5%)
    pallas_call x1, Pallas kernels, shards(): pl.pallas_call(functools.partial(kernel, dims), out_shape=[jax.ShapeDtype...  124 us
    unnamed x12, local copies, waits for them, and re-layouts  6.78 us

profile of v6, /device:TPU:97, one launch (start us, length us, event | category | flops | bytes accessed | tf_op | source)
XLA Modules:
  0.0 131.3 jit_solution(12146043841336933070)
XLA Ops:
  0.6 123.9 %experts.1 = (bf16[64,384]{1,0:T(8,128)(2,1)}, bf16[64,384]{1,0:T(8,128)(2,1)}, f32[1,64]{1,0:T(1,128)}, f32[32,1024]{1,0:T(8,128)}, bf16[1024,256]{1,0:T(8,128)(2,1)}, /*index=5*/bf16[256,1024]{1,0:T(8,128)(2,1)}) custom-call(bf16[384,1024]{1,0:T(8,128)(2,1)} %frames.1, f32[1,1024]{1,0:T(1,128)} %bitcast.21, f32[32,1024]{1,0:T(8,128)} %bitcast.16, ...), custom_call_target="tpu_custom_call" | custom-call | tf_op jit(solution)/shard_map/experts/pallas_call | solution.py:735
  124.5 0.0 copy-start.1
  124.5 1.5 %copy.19 = bf16[384,64]{0,1:T(8,128)(2,1)} copy(bf16[384,64]{0,1:T(8,128)(2,1)} %bitcast.19) | data formatting | bytes 98304
  126.0 0.0 copy-start.2
  126.0 1.4 %copy.20 = bf16[384,64]{0,1:T(8,128)(2,1)} copy(bf16[384,64]{0,1:T(8,128)(2,1)} %bitcast.18) | data formatting | bytes 98304
  127.4 0.0 copy-done.2
  127.4 0.5 copy.21
  127.9 0.0 copy-done.1
  127.9 0.7 copy.22
  128.6 0.0 copy-start
  128.6 1.9 %copy.23 = bf16[1,1024,256]{2,1,0:T(8,128)(2,1)} copy(bf16[1,1024,256]{2,1,0:T(8,128)(2,1)} %bitcast.13) | data formatting | bytes 1048576
  130.5 0.0 copy-done
  130.5 0.8 copy.24
Async XLA Ops:
  124.5 3.4 %copy-start.1 = (f32[32,1024]{1,0:T(8,128)S(1)}, f32[32,1024]{1,0:T(8,128)}, u32[]{:S(2)}) copy-start(f32[32,1024]{1,0:T(8,128)} %get-tuple-element.15) | copy-start | bytes 393220
  126.0 1.4 %copy-start.2 = (f32[1,64]{1,0:T(1,128)S(1)}, f32[1,64]{1,0:T(1,128)}, u32[]{:S(2)}) copy-start(f32[1,64]{1,0:T(1,128)} %get-tuple-element.14) | copy-start | bytes 772
  128.6 1.9 %copy-start = (bf16[256,1024]{1,0:T(8,128)(2,1)S(1)}, bf16[256,1024]{1,0:T(8,128)(2,1)}, u32[]{:S(2)}) copy-start(bf16[256,1024]{1,0:T(8,128)(2,1)} %get-tuple-element.17) | copy-start | bytes 1572868
